TPU v7x, 32 devices: a whole 2x2x4 slice. The times are simulated.
32 devices in a mesh: ctx: 8 (over y, x, core), head: 4 (over z).
Axes of the slice: x: 2, y: 2, z: 4, core: 2. Of those that a mesh axis runs over, the one named last changes fastest.
Arguments:
- query_latent: bfloat16 [2048, 1536], P(('ctx', 'head')), may hold values from -6 to 6
- norm_gain: bfloat16 [1536], replicated, may hold values from 0.099609375 to 1.8984375
- kv_latent: bfloat16 [2048, 576], P(('ctx', 'head')), may hold values from -120 to 120
- q_up: bfloat16 [1536, 3072], P(None, 'head'), may hold values from -0.15625 to 0.15625
- absorb_key: bfloat16 [16, 128, 512], P('head'), may hold values from -0.5 to 0.5
- absorb_value: bfloat16 [16, 512, 128], P('head'), may hold values from -0.25 to 0.25
- block_owner: int32 [8], replicated, may hold values from 0 to 7, each once
Outputs:
- head_output: bfloat16 [2048, 2048], P('ctx', 'head')
All inputs are finite; a program needn't handle non-finite values.
Results may differ from a plain program's by a relative error of at most 0.024.
The roundings to bfloat16 on the way count: a program that leaves them out, or rounds other values in their place, can miss the bound.
Values may be sent and summed in bfloat16 or wider, within the bound.
A program may use at most 64 MiB of HBM per device.

v0:
```python
import math

import jax
import jax.numpy as jnp
from jax import lax
from jax.sharding import PartitionSpec as P

epsilon = 1e-06
masked_score = -1e30


def rotate(values, positions):
    half_width = values.shape[-1] // 2
    frequency = jnp.exp(
        jnp.arange(half_width, dtype=jnp.float32) * (-math.log(10000.0) / half_width)
    )
    angles = positions.astype(jnp.float32)[:, None, None] * frequency
    cosine = jnp.cos(angles)
    sine = jnp.sin(angles)
    front = values[..., :half_width]
    back = values[..., half_width:]
    return jnp.concatenate([front * cosine - back * sine, front * sine + back * cosine], axis=-1)


def per_device(query_latent, norm_gain, kv_latent, q_up, absorb_key, absorb_value, block_owner):
    tok_dev = lax.axis_size("head") * query_latent.shape[0]
    half_len = tok_dev // 2
    ctx_count = lax.axis_size("ctx")
    head_count = absorb_key.shape[0]
    nope_width = absorb_key.shape[1]
    latent_width = absorb_key.shape[2]
    rope_width = q_up.shape[1] // head_count - nope_width
    kv_width = latent_width + rope_width
    score_scale = float(nope_width + rope_width) ** (-0.5)
    ctx_ids = jnp.arange(ctx_count, dtype=jnp.int32)

    def positions_of(row_ids):
        device = row_ids // tok_dev
        owner_ctx = jnp.sum(
            jnp.where(device[:, None] == ctx_ids[None, :], block_owner[None, :], 0), axis=1
        )
        offset = row_ids % tok_dev
        half_block = jnp.where(offset // half_len == 0, owner_ctx, 2 * ctx_count - 1 - owner_ctx)
        return half_block * half_len + offset % half_len

    block_begin = lax.axis_index("ctx") * tok_dev
    query_f32 = query_latent.astype(jnp.float32)
    normed = (
        query_f32
        * lax.rsqrt(jnp.mean(query_f32 * query_f32, axis=-1, keepdims=True) + epsilon)
        * norm_gain.astype(jnp.float32)
    ).astype(jnp.bfloat16)
    row_block = lax.all_gather(normed, "head", axis=0, tiled=True)
    row_count = row_block.shape[0]
    projected = jnp.dot(row_block, q_up, preferred_element_type=jnp.float32)
    projected = projected.reshape(row_count, head_count, nope_width + rope_width)
    q_nope = projected[..., :nope_width].astype(jnp.bfloat16)
    row_places = positions_of(block_begin + jnp.arange(row_count, dtype=jnp.int32))
    q_pe = rotate(projected[..., nope_width:], row_places).astype(jnp.bfloat16)
    q_abs = jnp.einsum(
        "thn,hnc->thc", q_nope, absorb_key, preferred_element_type=jnp.float32
    ).astype(jnp.bfloat16)
    queries = jnp.concatenate([q_abs, q_pe], axis=-1).reshape(row_count * head_count, kv_width)
    query_positions = jnp.repeat(
        positions_of(block_begin + jnp.arange(tok_dev, dtype=jnp.int32)), head_count
    )

    def attend_tile(running, key_rows, key_positions, query_rows, query_places):
        row_peak, row_total, weighted = running
        scores = jnp.dot(query_rows, key_rows.T, preferred_element_type=jnp.float32) * score_scale
        allowed = key_positions[None, :] <= query_places[:, None]
        scores = jnp.where(allowed, scores, masked_score)
        new_peak = jnp.maximum(row_peak, jnp.max(scores, axis=-1))
        weights = jnp.where(allowed, jnp.exp(scores - new_peak[:, None]), 0.0)
        rescale = jnp.exp(row_peak - new_peak)
        row_total = row_total * rescale + jnp.sum(weights, axis=-1)
        weighted = weighted * rescale[:, None] + jnp.dot(
            weights.astype(jnp.bfloat16),
            key_rows[:, :latent_width],
            preferred_element_type=jnp.float32,
        )
        return (new_peak, row_total, weighted)

    def visit(running, key_rows, key_positions):
        return attend_tile(running, key_rows, key_positions, queries, query_positions)

    query_count = tok_dev * head_count
    initial = (
        jnp.full((query_count,), masked_score, jnp.float32),
        jnp.zeros((query_count,), jnp.float32),
        jnp.zeros((query_count, latent_width), jnp.float32),
    )
    group_rows = lax.all_gather(kv_latent, "head", axis=0, tiled=True)
    running = initial
    key_block = lax.all_gather(group_rows, "ctx", axis=0, tiled=True)
    row_count = key_block.shape[0]
    sub_blocks = key_block.reshape(row_count // 256, 256, kv_width)
    block_starts = 256 * jnp.arange(row_count // 256, dtype=jnp.int32)

    def scan_step(state_in, element):
        key_places = positions_of(element[1] + jnp.arange(256, dtype=jnp.int32))
        return (visit(state_in, element[0], key_places), None)

    running, _ = lax.scan(scan_step, running, (sub_blocks, block_starts))
    row_peak, row_total, weighted = running
    latent_out = (
        (weighted / row_total[:, None])
        .astype(jnp.bfloat16)
        .reshape(tok_dev, head_count, latent_width)
    )
    head_output = jnp.einsum(
        "thc,hcv->thv", latent_out, absorb_value, preferred_element_type=jnp.float32
    )
    return head_output.astype(jnp.bfloat16).reshape(tok_dev, head_count * absorb_value.shape[2])


def solution(mesh):
    return jax.shard_map(
        per_device,
        mesh=mesh,
        in_specs=(
            P(("ctx", "head"), None),
            P(),
            P(("ctx", "head"), None),
            P(None, "head"),
            P("head", None, None),
            P("head", None, None),
            P(),
        ),
        out_specs=P("ctx", "head"),
        check_vma=False,
    )
```

profile of v0, /device:TPU:0, one launch (start us, length us, event | category | flops | bytes accessed | tf_op | source)
XLA Modules:
  0.0 145.9 jit_solution(12533644661428285931)
XLA Ops:
  6.5 18.0 %all_gather.9 = bf16[256,576]{1,0:T(8,128)(2,1)} all-gather(bf16[64,576]{1,0:T(8,128)(2,1)} %param.11), channel_id=1, replica_groups=mesh['ctx'=8,'head'=4] {'head'}, dimensions={0}, use_global_device_ids=true | all-gather | bytes 368640 | tf_op jit(solution)/shard_map/all_gather | solution.py:93
  27.4 17.4 %all_gather.11 = bf16[256,1536]{1,0:T(8,128)(2,1)S(1)} all-gather(bf16[64,1536]{1,0:T(8,128)(2,1)S(1)} %fusion.23), channel_id=1, replica_groups=mesh['ctx'=8,'head'=4] {'head'}, dimensions={0}, use_global_device_ids=true | all-gather | bytes 983040 | tf_op jit(solution)/shard_map/all_gather | solution.py:53
  49.1 2.1 %copy.34 = bf16[256,4,576]{2,1,0:T(4,128)(2,1)} copy(bf16[256,4,576]{2,0,1:T(8,128)(2,1)S(1)} %pad_maximum_fusion) | data formatting | bytes 2359296 | tf_op jit(solution)/shard_map/concatenate | solution.py:63
  51.2 3.4 %reshape.222 = bf16[1024,576]{1,0:T(8,128)(2,1)} reshape(bf16[256,4,576]{2,1,0:T(4,128)(2,1)} %copy.34) | data formatting | bytes 2359296 | tf_op jit(solution)/shard_map/reshape | solution.py:63
  54.8 78.6 %while.18 = (s32[]{:T(128)}, f32[1024]{0:T(1024)S(1)}, f32[1024]{0:T(1024)S(1)}, f32[1024,512]{1,0:T(8,128)}, s32[8]{0:T(128)S(1)}, /*index=5*/s32[8]{0:T(128)S(...) while((s32[]{:T(128)}, f32[1024]{0:T(1024)S(1)}, ...), condition=%wide.region_6.7_spmd.clone, body=%wide.region_2.6_spmd.clone.sunk | while | flops 575168256 | bytes 9766065 | solution.py:104
  56.8 1.7 %dynamic-slice_bitcast_fusion.2 = bf16[256,576]{1,0:T(8,128)(2,1)} fusion(bf16[8,256,576]{2,1,0:T(8,128)(2,1)} %get-tuple-element.333, s32[]{:T(128)} %get-tuple-element.316), kind=kLoop, calls=%fused_computation.14.clone.1 | loop fusion | bytes 589828 | tf_op jit(solution)/shard_map/while/body/jit(dynamic_index_in_dim)/squeeze | solution.py:104
  58.7 2.1 %fusion.51 = (f32[1024]{0:T(1024)S(1)}, f32[1024,256]{0,1:T(8,128)S(1)}) fusion(bf16[256,576]{1,0:T(8,128)(2,1)} %dynamic-slice_bitcast_fusion.2, bf16[1024,576]{1,0:T(8,128)(2,1)} %get-tuple-element.334, s32[1024]{0:T(1024)S(1)} %le.68, s32[256]{0:T(256)S(1)} %fusion.50), kind=kOutput, calls=%fused_computation.75.clone.1 | convolution fusion | flops 303037440 | bytes 2532352 | tf_op jit(solution)/shard_map/while/body/eval_jaxpr/dot_general | solution.py:70
  61.1 2.9 %fusion.54 = f32[1024,512]{1,0:T(8,128)} fusion(f32[1024,512]{1,0:T(8,128)} %get-tuple-element.319, f32[1024]{0:T(1024)S(1)} %get-tuple-element.304, pred[]{:T(512)S(6)} %compare.55, f32[1024,256]{0,1:T(8,128)S(1)} %get-tuple-element.302, f32[1024]{0:T(1024)S(1)} %select_maximum_fusion.2, s32[1024]{0:T(1024)S(1)} %le.68, s32[256]{0:T(256)S(1)} %fusion.50, ...), kind=kOutput, calls=%fused_computation.3.clone.1 | convolution fusion | flops 271056896 | bytes 5518337 | tf_op jit(solution)/shard_map/while/body/eval_jaxpr/dot_general | solution.py:77
  66.0 1.7 %dynamic-slice_bitcast_fusion.2 = bf16[256,576]{1,0:T(8,128)(2,1)} fusion(bf16[8,256,576]{2,1,0:T(8,128)(2,1)} %get-tuple-element.333, s32[]{:T(128)} %get-tuple-element.316), kind=kLoop, calls=%fused_computation.14.clone.1 | loop fusion | bytes 589828 | tf_op jit(solution)/shard_map/while/body/jit(dynamic_index_in_dim)/squeeze | solution.py:104
  67.9 2.1 %fusion.51 = (f32[1024]{0:T(1024)S(1)}, f32[1024,256]{0,1:T(8,128)S(1)}) fusion(bf16[256,576]{1,0:T(8,128)(2,1)} %dynamic-slice_bitcast_fusion.2, bf16[1024,576]{1,0:T(8,128)(2,1)} %get-tuple-element.334, s32[1024]{0:T(1024)S(1)} %le.68, s32[256]{0:T(256)S(1)} %fusion.50), kind=kOutput, calls=%fused_computation.75.clone.1 | convolution fusion | flops 303037440 | bytes 2532352 | tf_op jit(solution)/shard_map/while/body/eval_jaxpr/dot_general | solution.py:70
  70.3 3.6 %fusion.54 = f32[1024,512]{1,0:T(8,128)} fusion(f32[1024,512]{1,0:T(8,128)} %get-tuple-element.319, f32[1024]{0:T(1024)S(1)} %get-tuple-element.304, pred[]{:T(512)S(6)} %compare.55, f32[1024,256]{0,1:T(8,128)S(1)} %get-tuple-element.302, f32[1024]{0:T(1024)S(1)} %select_maximum_fusion.2, s32[1024]{0:T(1024)S(1)} %le.68, s32[256]{0:T(256)S(1)} %fusion.50, ...), kind=kOutput, calls=%fused_computation.3.clone.1 | convolution fusion | flops 271056896 | bytes 5518337 | tf_op jit(solution)/shard_map/while/body/eval_jaxpr/dot_general | solution.py:77
  75.9 1.7 %dynamic-slice_bitcast_fusion.2 = bf16[256,576]{1,0:T(8,128)(2,1)} fusion(bf16[8,256,576]{2,1,0:T(8,128)(2,1)} %get-tuple-element.333, s32[]{:T(128)} %get-tuple-element.316), kind=kLoop, calls=%fused_computation.14.clone.1 | loop fusion | bytes 589828 | tf_op jit(solution)/shard_map/while/body/jit(dynamic_index_in_dim)/squeeze | solution.py:104
  77.9 2.1 %fusion.51 = (f32[1024]{0:T(1024)S(1)}, f32[1024,256]{0,1:T(8,128)S(1)}) fusion(bf16[256,576]{1,0:T(8,128)(2,1)} %dynamic-slice_bitcast_fusion.2, bf16[1024,576]{1,0:T(8,128)(2,1)} %get-tuple-element.334, s32[1024]{0:T(1024)S(1)} %le.68, s32[256]{0:T(256)S(1)} %fusion.50), kind=kOutput, calls=%fused_computation.75.clone.1 | convolution fusion | flops 303037440 | bytes 2532352 | tf_op jit(solution)/shard_map/while/body/eval_jaxpr/dot_general | solution.py:70
  80.2 3.6 %fusion.54 = f32[1024,512]{1,0:T(8,128)} fusion(f32[1024,512]{1,0:T(8,128)} %get-tuple-element.319, f32[1024]{0:T(1024)S(1)} %get-tuple-element.304, pred[]{:T(512)S(6)} %compare.55, f32[1024,256]{0,1:T(8,128)S(1)} %get-tuple-element.302, f32[1024]{0:T(1024)S(1)} %select_maximum_fusion.2, s32[1024]{0:T(1024)S(1)} %le.68, s32[256]{0:T(256)S(1)} %fusion.50, ...), kind=kOutput, calls=%fused_computation.3.clone.1 | convolution fusion | flops 271056896 | bytes 5518337 | tf_op jit(solution)/shard_map/while/body/eval_jaxpr/dot_general | solution.py:77
  85.8 1.7 %dynamic-slice_bitcast_fusion.2 = bf16[256,576]{1,0:T(8,128)(2,1)} fusion(bf16[8,256,576]{2,1,0:T(8,128)(2,1)} %get-tuple-element.333, s32[]{:T(128)} %get-tuple-element.316), kind=kLoop, calls=%fused_computation.14.clone.1 | loop fusion | bytes 589828 | tf_op jit(solution)/shard_map/while/body/jit(dynamic_index_in_dim)/squeeze | solution.py:104
  87.8 2.1 %fusion.51 = (f32[1024]{0:T(1024)S(1)}, f32[1024,256]{0,1:T(8,128)S(1)}) fusion(bf16[256,576]{1,0:T(8,128)(2,1)} %dynamic-slice_bitcast_fusion.2, bf16[1024,576]{1,0:T(8,128)(2,1)} %get-tuple-element.334, s32[1024]{0:T(1024)S(1)} %le.68, s32[256]{0:T(256)S(1)} %fusion.50), kind=kOutput, calls=%fused_computation.75.clone.1 | convolution fusion | flops 303037440 | bytes 2532352 | tf_op jit(solution)/shard_map/while/body/eval_jaxpr/dot_general | solution.py:70
  90.1 3.6 %fusion.54 = f32[1024,512]{1,0:T(8,128)} fusion(f32[1024,512]{1,0:T(8,128)} %get-tuple-element.319, f32[1024]{0:T(1024)S(1)} %get-tuple-element.304, pred[]{:T(512)S(6)} %compare.55, f32[1024,256]{0,1:T(8,128)S(1)} %get-tuple-element.302, f32[1024]{0:T(1024)S(1)} %select_maximum_fusion.2, s32[1024]{0:T(1024)S(1)} %le.68, s32[256]{0:T(256)S(1)} %fusion.50, ...), kind=kOutput, calls=%fused_computation.3.clone.1 | convolution fusion | flops 271056896 | bytes 5518337 | tf_op jit(solution)/shard_map/while/body/eval_jaxpr/dot_general | solution.py:77
  95.7 1.7 %dynamic-slice_bitcast_fusion.2 = bf16[256,576]{1,0:T(8,128)(2,1)} fusion(bf16[8,256,576]{2,1,0:T(8,128)(2,1)} %get-tuple-element.333, s32[]{:T(128)} %get-tuple-element.316), kind=kLoop, calls=%fused_computation.14.clone.1 | loop fusion | bytes 589828 | tf_op jit(solution)/shard_map/while/body/jit(dynamic_index_in_dim)/squeeze | solution.py:104
  97.7 2.1 %fusion.51 = (f32[1024]{0:T(1024)S(1)}, f32[1024,256]{0,1:T(8,128)S(1)}) fusion(bf16[256,576]{1,0:T(8,128)(2,1)} %dynamic-slice_bitcast_fusion.2, bf16[1024,576]{1,0:T(8,128)(2,1)} %get-tuple-element.334, s32[1024]{0:T(1024)S(1)} %le.68, s32[256]{0:T(256)S(1)} %fusion.50), kind=kOutput, calls=%fused_computation.75.clone.1 | convolution fusion | flops 303037440 | bytes 2532352 | tf_op jit(solution)/shard_map/while/body/eval_jaxpr/dot_general | solution.py:70
  100.0 3.6 %fusion.54 = f32[1024,512]{1,0:T(8,128)} fusion(f32[1024,512]{1,0:T(8,128)} %get-tuple-element.319, f32[1024]{0:T(1024)S(1)} %get-tuple-element.304, pred[]{:T(512)S(6)} %compare.55, f32[1024,256]{0,1:T(8,128)S(1)} %get-tuple-element.302, f32[1024]{0:T(1024)S(1)} %select_maximum_fusion.2, s32[1024]{0:T(1024)S(1)} %le.68, s32[256]{0:T(256)S(1)} %fusion.50, ...), kind=kOutput, calls=%fused_computation.3.clone.1 | convolution fusion | flops 271056896 | bytes 5518337 | tf_op jit(solution)/shard_map/while/body/eval_jaxpr/dot_general | solution.py:77
  105.7 1.7 %dynamic-slice_bitcast_fusion.2 = bf16[256,576]{1,0:T(8,128)(2,1)} fusion(bf16[8,256,576]{2,1,0:T(8,128)(2,1)} %get-tuple-element.333, s32[]{:T(128)} %get-tuple-element.316), kind=kLoop, calls=%fused_computation.14.clone.1 | loop fusion | bytes 589828 | tf_op jit(solution)/shard_map/while/body/jit(dynamic_index_in_dim)/squeeze | solution.py:104
  107.6 2.1 %fusion.51 = (f32[1024]{0:T(1024)S(1)}, f32[1024,256]{0,1:T(8,128)S(1)}) fusion(bf16[256,576]{1,0:T(8,128)(2,1)} %dynamic-slice_bitcast_fusion.2, bf16[1024,576]{1,0:T(8,128)(2,1)} %get-tuple-element.334, s32[1024]{0:T(1024)S(1)} %le.68, s32[256]{0:T(256)S(1)} %fusion.50), kind=kOutput, calls=%fused_computation.75.clone.1 | convolution fusion | flops 303037440 | bytes 2532352 | tf_op jit(solution)/shard_map/while/body/eval_jaxpr/dot_general | solution.py:70
  110.0 3.6 %fusion.54 = f32[1024,512]{1,0:T(8,128)} fusion(f32[1024,512]{1,0:T(8,128)} %get-tuple-element.319, f32[1024]{0:T(1024)S(1)} %get-tuple-element.304, pred[]{:T(512)S(6)} %compare.55, f32[1024,256]{0,1:T(8,128)S(1)} %get-tuple-element.302, f32[1024]{0:T(1024)S(1)} %select_maximum_fusion.2, s32[1024]{0:T(1024)S(1)} %le.68, s32[256]{0:T(256)S(1)} %fusion.50, ...), kind=kOutput, calls=%fused_computation.3.clone.1 | convolution fusion | flops 271056896 | bytes 5518337 | tf_op jit(solution)/shard_map/while/body/eval_jaxpr/dot_general | solution.py:77
  115.6 1.7 %dynamic-slice_bitcast_fusion.2 = bf16[256,576]{1,0:T(8,128)(2,1)} fusion(bf16[8,256,576]{2,1,0:T(8,128)(2,1)} %get-tuple-element.333, s32[]{:T(128)} %get-tuple-element.316), kind=kLoop, calls=%fused_computation.14.clone.1 | loop fusion | bytes 589828 | tf_op jit(solution)/shard_map/while/body/jit(dynamic_index_in_dim)/squeeze | solution.py:104
  117.5 2.1 %fusion.51 = (f32[1024]{0:T(1024)S(1)}, f32[1024,256]{0,1:T(8,128)S(1)}) fusion(bf16[256,576]{1,0:T(8,128)(2,1)} %dynamic-slice_bitcast_fusion.2, bf16[1024,576]{1,0:T(8,128)(2,1)} %get-tuple-element.334, s32[1024]{0:T(1024)S(1)} %le.68, s32[256]{0:T(256)S(1)} %fusion.50), kind=kOutput, calls=%fused_computation.75.clone.1 | convolution fusion | flops 303037440 | bytes 2532352 | tf_op jit(solution)/shard_map/while/body/eval_jaxpr/dot_general | solution.py:70
  119.9 3.6 %fusion.54 = f32[1024,512]{1,0:T(8,128)} fusion(f32[1024,512]{1,0:T(8,128)} %get-tuple-element.319, f32[1024]{0:T(1024)S(1)} %get-tuple-element.304, pred[]{:T(512)S(6)} %compare.55, f32[1024,256]{0,1:T(8,128)S(1)} %get-tuple-element.302, f32[1024]{0:T(1024)S(1)} %select_maximum_fusion.2, s32[1024]{0:T(1024)S(1)} %le.68, s32[256]{0:T(256)S(1)} %fusion.50, ...), kind=kOutput, calls=%fused_computation.3.clone.1 | convolution fusion | flops 271056896 | bytes 5518337 | tf_op jit(solution)/shard_map/while/body/eval_jaxpr/dot_general | solution.py:77
  125.5 1.7 %dynamic-slice_bitcast_fusion.2 = bf16[256,576]{1,0:T(8,128)(2,1)} fusion(bf16[8,256,576]{2,1,0:T(8,128)(2,1)} %get-tuple-element.333, s32[]{:T(128)} %get-tuple-element.316), kind=kLoop, calls=%fused_computation.14.clone.1 | loop fusion | bytes 589828 | tf_op jit(solution)/shard_map/while/body/jit(dynamic_index_in_dim)/squeeze | solution.py:104
  127.5 2.1 %fusion.51 = (f32[1024]{0:T(1024)S(1)}, f32[1024,256]{0,1:T(8,128)S(1)}) fusion(bf16[256,576]{1,0:T(8,128)(2,1)} %dynamic-slice_bitcast_fusion.2, bf16[1024,576]{1,0:T(8,128)(2,1)} %get-tuple-element.334, s32[1024]{0:T(1024)S(1)} %le.68, s32[256]{0:T(256)S(1)} %fusion.50), kind=kOutput, calls=%fused_computation.75.clone.1 | convolution fusion | flops 303037440 | bytes 2532352 | tf_op jit(solution)/shard_map/while/body/eval_jaxpr/dot_general | solution.py:70
  129.8 3.6 %fusion.54 = f32[1024,512]{1,0:T(8,128)} fusion(f32[1024,512]{1,0:T(8,128)} %get-tuple-element.319, f32[1024]{0:T(1024)S(1)} %get-tuple-element.304, pred[]{:T(512)S(6)} %compare.55, f32[1024,256]{0,1:T(8,128)S(1)} %get-tuple-element.302, f32[1024]{0:T(1024)S(1)} %select_maximum_fusion.2, s32[1024]{0:T(1024)S(1)} %le.68, s32[256]{0:T(256)S(1)} %fusion.50, ...), kind=kOutput, calls=%fused_computation.3.clone.1 | convolution fusion | flops 271056896 | bytes 5518337 | tf_op jit(solution)/shard_map/while/body/eval_jaxpr/dot_general | solution.py:77
  133.4 1.8 %divide_convert_fusion = bf16[1024,512]{1,0:T(8,128)(2,1)S(1)} fusion(f32[1024,512]{1,0:T(8,128)} %get-tuple-element.175, f32[1024]{0:T(1024)S(1)} %get-tuple-element.176), kind=kLoop, calls=%fused_computation.38 | loop fusion | flops 1048576 | bytes 3149824 | tf_op jit(solution)/shard_map/convert_element_type | solution.py:108
  135.2 1.1 reshape.223
  136.4 1.8 %convolution_convert_fusion.1 = bf16[4,256,128]{1,2,0:T(8,128)(2,1)S(1)} fusion(bf16[4,512,128]{2,1,0:T(8,128)(2,1)} %param.14, bf16[256,4,512]{2,1,0:T(4,128)(2,1)} %reshape.223), kind=kOutput, calls=%fused_computation.42 | convolution fusion | flops 134348800 | bytes 1835008 | tf_op jit(solution)/shard_map/thc,hcv->thv/dot_general | solution.py:111
  (114 shorter events, 27.6 us)
Async XLA Ops:
  6.5 38.3 %copy-start = (bf16[1536,768]{1,0:T(8,128)(2,1)S(1)}, bf16[1536,768]{1,0:T(8,128)(2,1)}, u32[]{:S(2)}) copy-start(bf16[1536,768]{1,0:T(8,128)(2,1)} %param.12) | copy-start | bytes 7077892
  6.5 48.3 %all-gather.2.cloned.1.call-start = ((), (), s32[]{:S(2)}) async-start(), calls=%async_computation | async-start | bytes 2949120 | tf_op jit(solution)/shard_map/all_gather | solution.py:95
  44.8 2.4 %copy-start.4 = (s32[8]{0:T(128)S(1)}, s32[8]{0:T(128)}, u32[]{:S(2)}) copy-start(s32[8]{0:T(128)} %param.15) | copy-start | bytes 100
  45.8 0.9 copy-start.1
  47.1 1.1 copy-start.2
  47.2 1.3 copy-start.3
Sparse Core Ops, SparseCore 0:
  24.6 30.1 all-gather.1
where the time goes:
time: 147 us; the launch traced here: 146 us
  matrix products  48.2 us (33%)
  blocking collectives  35.4 us (24%)
  local copies, waits for them, and re-layouts  29.6 us (20%)
  other arithmetic  18.7 us (13%)
  between operations  13.6 us (9%)
    dot_general x8, matrix products, attend_tile(): jnp.dot(weights.astype(jnp.bfloat16), key_rows[:, :latent_width], preferr...  28.3 us
    all_gather x1, blocking collectives, per_device(): group_rows = lax.all_gather(kv_latent, 'head', axis=0, tiled=True)  18 us
    all_gather x1, blocking collectives, per_device(): row_block = lax.all_gather(normed, 'head', axis=0, tiled=True)  17.4 us
    dot_general x8, matrix products, attend_tile(): jnp.dot(query_rows, key_rows.T, preferred_element_type=jnp.float32)  16.5 us
    squeeze x8, local copies, waits for them, and re-layouts, per_device(): running, _ = lax.scan(scan_step, running, (sub_blocks, block_starts))  13.8 us
    add x8, other arithmetic, positions_of(): return half_block * half_len + offset % half_len  5.21 us
    select_n x9, other arithmetic, positions_of(): device = row_ids // tok_dev  5.13 us
    dynamic_slice x8, local copies, waits for them, and re-layouts, per_device(): running, _ = lax.scan(scan_step, running, (sub_blocks, block_starts))  4.85 us
  transfers between devices with their start and end apart: 1, of which 1 were waited for; matrix products, arithmetic and copies ran while one was open for 8% of the time, Pallas kernels for 0%

commit v1 on v0

v1 whole, which is shorter than its diff:
```python
import functools
import math

import jax
import jax.numpy as jnp
from jax import lax
from jax.experimental import pallas as pl
from jax.experimental.pallas import tpu as pltpu
from jax.sharding import PartitionSpec as P

epsilon = 1e-06
masked_score = -1e30
MESH = pl.DeviceIdType.MESH


def when(condition, action):
    if condition is True:
        action()
    else:
        pl.when(condition)(action)


def both(first, second):
    if first is True:
        return second
    if second is True:
        return first
    return jnp.logical_and(first, second)


def kernel(
    ctx_count,
    head_devices,
    owner_ref,
    query_ref,
    gain_ref,
    kv_ref,
    q_up_hbm,
    absorb_key_hbm,
    absorb_value_hbm,
    out_ref,
    q_up_ref,
    absorb_key_ref,
    absorb_value_ref,
    kv_all,
    normed_all,
    cosine_ref,
    sine_ref,
    key_pos_ref,
    projected_ref,
    queries_ref,
    kv_recv,
    kv_send,
    norm_recv,
    norm_send_up,
    norm_send_down,
    load_sem,
):
    rows = query_ref.shape[0]
    head_count, nope_width, latent_width = absorb_key_ref.shape
    value_width = absorb_value_ref.shape[2]
    head_width = q_up_ref.shape[1] // head_count
    rope_width = head_width - nope_width
    half_width = rope_width // 2
    tok_dev = rows * head_devices
    half_len = tok_dev // 2
    chips = ctx_count // 2
    bits = chips.bit_length() - 1
    last = head_devices - 1
    ctx = lax.axis_index("ctx")
    z = lax.axis_index("head")

    def across(relative):
        place = ctx
        for bit in range(bits):
            if (relative >> bit) & 1:
                weight = 2 ** (bit + 1)
                place = place + weight - 2 * weight * lax.rem(lax.div(ctx, weight), 2)
        return place

    def other_core(place):
        return place + 1 - 2 * lax.rem(place, 2)

    sibling = other_core(ctx)

    loads = [
        pltpu.make_async_copy(q_up_hbm, q_up_ref, load_sem.at[0]),
        pltpu.make_async_copy(absorb_key_hbm, absorb_key_ref, load_sem.at[1]),
        pltpu.make_async_copy(absorb_value_hbm, absorb_value_ref, load_sem.at[2]),
    ]

    barrier = pltpu.get_barrier_semaphore()
    for bit in range(bits):
        pl.semaphore_signal(barrier, inc=1, device_id=(across(1 << bit), z), device_id_type=MESH)
    pl.semaphore_signal(barrier, inc=1, device_id=(sibling, z), device_id_type=MESH)

    @pl.when(z > 0)
    def _():
        pl.semaphore_signal(barrier, inc=1, device_id=(ctx, z - 1), device_id_type=MESH)

    @pl.when(z < last)
    def _():
        pl.semaphore_signal(barrier, inc=1, device_id=(ctx, z + 1), device_id_type=MESH)

    for load in loads:
        load.start()
    kv_all[ctx * head_devices + z] = kv_ref[...]
    pl.semaphore_wait(
        barrier, bits + 1 + jnp.where(z > 0, 1, 0) + jnp.where(z < last, 1, 0)
    )

    sent = []

    def kv_copy(origin, piece, slot, target):
        index = origin * head_devices + piece
        return pltpu.make_async_remote_copy(
            src_ref=kv_all.at[index],
            dst_ref=kv_all.at[index],
            send_sem=kv_send.at[slot],
            recv_sem=kv_recv.at[index],
            device_id=target,
            device_id_type=MESH,
        )

    def send_kv(condition, origin, piece, target):
        copy = kv_copy(origin, piece, len(sent), target)
        sent.append((condition, copy))
        when(condition, copy.start)

    def wait_kv(condition, origin, piece):
        when(condition, kv_copy(origin, piece, 0, (sibling, z)).wait_recv)

    def pieces(step):
        if step == 0:
            return [(True, z, 0)]
        return [(z >= step, z - step, 1), (z + step <= last, z + step, -1)]

    def own_block(step):
        for valid, piece, way in pieces(step):
            if step > 0:
                wait_kv(valid, ctx, piece)
            if way >= 0 and step < last:
                send_kv(both(valid, z < last), ctx, piece, (ctx, z + 1))
            if way <= 0 and step < last:
                send_kv(both(valid, z > 0), ctx, piece, (ctx, z - 1))
            for bit in range(bits):
                send_kv(valid, ctx, piece, (across(1 << bit), z))
            send_kv(valid, ctx, piece, (sibling, z))

    def relay(step, relative):
        origin = across(relative)
        for valid, piece, _ in pieces(step):
            wait_kv(valid, origin, piece)
            even = lax.rem(piece + head_devices, 2) == 0
            for bit in range(bits):
                if relative < (1 << bit):
                    send_kv(both(valid, even), origin, piece, (across(1 << bit), z))
                elif relative & ((2 << bit) - 1) == 0:
                    odd = jnp.logical_not(even)
                    send_kv(both(valid, odd), origin, piece, (across(1 << bit), z))
            send_kv(valid, origin, piece, (sibling, z))

    def norm_copy(block, upward):
        send_sem, target = (
            (norm_send_up, z + 1) if upward else (norm_send_down, z - 1)
        )
        return pltpu.make_async_remote_copy(
            src_ref=normed_all.at[block],
            dst_ref=normed_all.at[block],
            send_sem=send_sem.at[block],
            recv_sem=norm_recv.at[block],
            device_id=(ctx, target),
            device_id_type=MESH,
        )

    def norm_step(step):
        @pl.when(z >= step)
        def _():
            norm_copy(z - step, True).wait_recv()

            @pl.when(z < last)
            def _():
                norm_copy(z - step, True).start()

        @pl.when(z + step <= last)
        def _():
            norm_copy(z + step, False).wait_recv()

            @pl.when(z > 0)
            def _():
                norm_copy(z + step, False).start()

    own_block(0)
    query_f32 = query_ref[...].astype(jnp.float32)
    normed_all[z] = (
        query_f32
        * lax.rsqrt(jnp.mean(query_f32 * query_f32, axis=-1, keepdims=True) + epsilon)
        * gain_ref[...].astype(jnp.float32)
    ).astype(jnp.bfloat16)

    def send_norm():
        @pl.when(z < last)
        def _():
            norm_copy(z, True).start()

        @pl.when(z > 0)
        def _():
            norm_copy(z, False).start()

    def half_base(owner, upper):
        return jnp.where(upper, 2 * ctx_count - 1 - owner, owner) * half_len

    def tables():
        own = owner_ref[ctx]
        offset = lax.broadcasted_iota(jnp.int32, (tok_dev, 1), 0)
        places = jnp.where(
            offset < half_len,
            own * half_len + offset,
            (2 * ctx_count - 1 - own) * half_len + offset - half_len,
        )
        frequency = jnp.exp(
            lax.broadcasted_iota(jnp.int32, (1, half_width), 1).astype(jnp.float32)
            * (-math.log(10000.0) / half_width)
        )
        angles = places.astype(jnp.float32) * frequency
        cosine_ref[...] = jnp.cos(angles).reshape(cosine_ref.shape)
        sine_ref[...] = jnp.sin(angles).reshape(sine_ref.shape)
        lane = lax.broadcasted_iota(jnp.int32, (1, half_len), 1)
        for index in range(ctx_count):
            owner = owner_ref[index]
            begin = index * tok_dev
            key_pos_ref[:, begin : begin + half_len] = owner * half_len + lane
            key_pos_ref[:, begin + half_len : begin + tok_dev] = (
                2 * ctx_count - 1 - owner
            ) * half_len + lane

    distances = [
        [r for r in range(chips) if bin(r).count("1") == level] for level in range(bits + 1)
    ]
    for stage in range(head_devices + bits):
        if 0 < stage < head_devices:
            own_block(stage)
        if stage == max(last - 1, 0):
            send_norm()
        for level in range(1, bits + 1):
            if 0 <= stage - level < head_devices:
                for relative in distances[level]:
                    relay(stage - level, relative)
        if stage == max(last - 1, 0):
            tables()
            for load in loads:
                load.wait()
        if stage == last and last > 0:
            norm_step(1)

    for relative in range(chips):
        for piece in range(head_devices):
            wait_kv(True, other_core(across(relative)), piece)

    factor = float(head_width) ** (-0.5) * math.log2(math.e)
    shorter = jnp.minimum(z, last - z)

    def block_body(step, carry):
        near = z + lax.div(step + 1, 2) * (1 - 2 * lax.rem(step, 2))
        far = jnp.where(z > last - z, last - step, step)
        block = jnp.where(step <= 2 * shorter, near, far)
        projected_ref[...] = jnp.dot(
            normed_all[block], q_up_ref[...], preferred_element_type=jnp.float32
        )
        cosine = cosine_ref[block]
        sine = sine_ref[block]
        for head in range(head_count):
            begin = head * head_width
            q_nope = projected_ref[:, begin : begin + nope_width].astype(jnp.bfloat16)
            q_abs = jnp.dot(q_nope, absorb_key_ref[head], preferred_element_type=jnp.float32)
            begin += nope_width
            front = projected_ref[:, begin : begin + half_width]
            back = projected_ref[:, begin + half_width : begin + rope_width]
            span = slice(head * rows, (head + 1) * rows)
            queries_ref[span, :latent_width] = q_abs.astype(jnp.bfloat16)
            queries_ref[span, latent_width:] = jnp.concatenate(
                [front * cosine - back * sine, front * sine + back * cosine], axis=-1
            ).astype(jnp.bfloat16)

        @pl.when(step + 2 <= last)
        def _():
            norm_step(step + 2)

        offset = block * rows
        base = half_base(owner_ref[ctx], offset >= half_len) + lax.rem(offset, half_len)
        query_pos = base + lax.rem(
            lax.broadcasted_iota(jnp.int32, (head_count * rows, 1), 0), rows
        )
        keys = kv_all[...].reshape(ctx_count * tok_dev, latent_width + rope_width)
        scores = lax.dot_general(
            queries_ref[...], keys, (((1,), (1,)), ((), ())), preferred_element_type=jnp.float32
        )
        scores = jnp.where(key_pos_ref[...] <= query_pos, scores, masked_score)
        peak = jnp.max(scores, axis=-1, keepdims=True)
        weights = jnp.exp2((scores - peak) * factor)
        total = jnp.sum(weights, axis=-1, keepdims=True)
        weighted = jnp.dot(
            weights.astype(jnp.bfloat16),
            keys[:, :latent_width],
            preferred_element_type=jnp.float32,
        )
        latent_out = (weighted / total).astype(jnp.bfloat16)
        for head in range(head_count):
            out_ref[block, :, head * value_width : (head + 1) * value_width] = jnp.dot(
                latent_out[head * rows : (head + 1) * rows],
                absorb_value_ref[head],
                preferred_element_type=jnp.float32,
            ).astype(jnp.bfloat16)
        return carry

    lax.fori_loop(0, head_devices, block_body, 0)

    for condition, copy in sent:
        when(condition, copy.wait_send)
    for block in range(head_devices):
        @pl.when(jnp.logical_and(z >= block, z < last))
        def _():
            norm_copy(block, True).wait_send()

        @pl.when(jnp.logical_and(z <= block, z > 0))
        def _():
            norm_copy(block, False).wait_send()


def per_device(query_latent, norm_gain, kv_latent, q_up, absorb_key, absorb_value, block_owner):
    head_devices = lax.axis_size("head")
    ctx_count = lax.axis_size("ctx")
    rows, query_width = query_latent.shape
    kv_width = kv_latent.shape[1]
    head_count, _, value_width = absorb_value.shape
    rope_half = (kv_width - absorb_key.shape[2]) // 2
    tok_dev = rows * head_devices
    piece_count = ctx_count * head_devices
    bits = (ctx_count // 2).bit_length() - 1
    slots = head_devices * ((ctx_count // 2) * (bits + 1) * 2 + 4)
    bf16, f32 = jnp.bfloat16, jnp.float32
    whole = pl.BlockSpec(memory_space=pltpu.VMEM)
    away = pl.BlockSpec(memory_space=pl.ANY)
    out = pl.pallas_call(
        functools.partial(kernel, ctx_count, head_devices),
        out_shape=jax.ShapeDtypeStruct((head_devices, rows, head_count * value_width), bf16),
        in_specs=[pl.BlockSpec(memory_space=pltpu.SMEM), whole, whole, whole, away, away, away],
        out_specs=whole,
        scratch_shapes=[
            pltpu.VMEM(q_up.shape, bf16),
            pltpu.VMEM(absorb_key.shape, bf16),
            pltpu.VMEM(absorb_value.shape, bf16),
            pltpu.VMEM((piece_count, rows, kv_width), bf16),
            pltpu.VMEM((head_devices, rows, query_width), bf16),
            pltpu.VMEM((head_devices, rows, rope_half), f32),
            pltpu.VMEM((head_devices, rows, rope_half), f32),
            pltpu.VMEM((1, ctx_count * tok_dev), jnp.int32),
            pltpu.VMEM((rows, q_up.shape[1]), f32),
            pltpu.VMEM((head_count * rows, kv_width), bf16),
            pltpu.SemaphoreType.DMA((piece_count,)),
            pltpu.SemaphoreType.DMA((slots,)),
            pltpu.SemaphoreType.DMA((head_devices,)),
            pltpu.SemaphoreType.DMA((head_devices,)),
            pltpu.SemaphoreType.DMA((head_devices,)),
            pltpu.SemaphoreType.DMA((3,)),
        ],
        compiler_params=pltpu.CompilerParams(
            collective_id=0, has_side_effects=True, vmem_limit_bytes=48 * 1024 * 1024
        ),
    )(
        block_owner,
        query_latent,
        norm_gain.reshape(1, query_width),
        kv_latent,
        q_up,
        absorb_key,
        absorb_value,
    )
    return out.reshape(tok_dev, head_count * value_width)


def solution(mesh):
    return jax.shard_map(
        per_device,
        mesh=mesh,
        in_specs=(
            P(("ctx", "head"), None),
            P(),
            P(("ctx", "head"), None),
            P(None, "head"),
            P("head", None, None),
            P("head", None, None),
            P(),
        ),
        out_specs=P("ctx", "head"),
        check_vma=False,
    )
```

time: 147 us -> 47.7 us (0.32)
  the two profiles are of different devices: /device:TPU:0 before, /device:TPU:1 now
where the time goes in v1:
time: 47.7 us; the launch traced here: 47.3 us
  Pallas kernels  39.7 us (83%)
  local copies, waits for them, and re-layouts  7.61 us (16%)
    pallas_call x1, Pallas kernels, per_device(): pl.pallas_call(functools.partial(kernel, ctx_count, head_devices), out_sh...  39.7 us
    unnamed x13, local copies, waits for them, and re-layouts  6.92 us

profile of v1, /device:TPU:1, one launch (start us, length us, event | category | flops | bytes accessed | tf_op | source)
XLA Modules:
  0.0 47.3 jit_solution(14618708985161572155)
XLA Ops:
  0.0 0.7 %reshape.6.gain_ref = bf16[1,1536]{1,0:T(2,128)(2,1)S(1)} reshape(bf16[1536]{0:T(1024)(128)(2,1)} %param.8) | data formatting | bytes 6144 | tf_op jit(solution)/shard_map/reshape | solution.py:373
  0.7 0.0 copy-start
  0.7 1.7 %copy-done = bf16[1536,768]{1,0:T(8,128)(2,1)S(1)} copy-done((bf16[1536,768]{1,0:T(8,128)(2,1)S(1)}, bf16[1536,768]{1,0:T(8,128)(2,1)}, u32[]{:S(2)}) %copy-start) | copy-done | bytes 2359320
  2.4 0.0 copy-start.1
  2.4 1.0 %copy-done.1 = bf16[4,128,512]{2,1,0:T(8,128)(2,1)S(1)} copy-done((bf16[4,128,512]{2,1,0:T(8,128)(2,1)S(1)}, bf16[4,128,512]{2,1,0:T(8,128)(2,1)}, u32[]{:S(2)}) %copy-start.1) | copy-done | bytes 524312
  3.4 0.0 copy-start.2
  3.4 1.0 %copy-done.2 = bf16[4,512,128]{2,1,0:T(8,128)(2,1)S(1)} copy-done((bf16[4,512,128]{2,1,0:T(8,128)(2,1)S(1)}, bf16[4,512,128]{2,1,0:T(8,128)(2,1)}, u32[]{:S(2)}) %copy-start.2) | copy-done | bytes 524312
  4.4 0.0 copy-start.3
  4.4 0.9 %copy-done.3 = bf16[64,1536]{1,0:T(8,128)(2,1)S(1)} copy-done((bf16[64,1536]{1,0:T(8,128)(2,1)S(1)}, bf16[64,1536]{1,0:T(8,128)(2,1)}, u32[]{:S(2)}) %copy-start.3) | copy-done | bytes 196632
  5.4 0.0 copy-start.4
  5.4 0.9 %copy-done.4 = bf16[64,576]{1,0:T(8,128)(2,1)S(1)} copy-done((bf16[64,576]{1,0:T(8,128)(2,1)S(1)}, bf16[64,576]{1,0:T(8,128)(2,1)}, u32[]{:S(2)}) %copy-start.4) | copy-done | bytes 73752
  6.3 0.0 copy-start.5
  6.3 0.7 %copy-done.5 = s32[8]{0:T(128)S(1)} copy-done((s32[8]{0:T(128)S(1)}, s32[8]{0:T(128)}, u32[]{:S(2)}) %copy-start.5) | copy-done | bytes 56
  6.9 39.7 %shard_map.73 = bf16[4,64,512]{2,1,0:T(8,128)(2,1)S(1)} custom-call(s32[8]{0:T(128)S(1)} %copy-done.5, bf16[64,1536]{1,0:T(8,128)(2,1)S(1)} %copy-done.3, bf16[1,1536]{1,0:T(2,128)(2,1)S(1)} %reshape.6.gain_ref, bf16[64,576]{1,0:T(8,128)(2,1)S(1)} %copy-done.4, bf16[1536,768]{1,0:T(8,128)(2,1)S(1)} %copy-done, bf16[4,128,512]{2,1,0:T(8,128)(2,1)S(1)} %copy-done.1, ...), custom_call_target="tpu_custom_call" | custom-call | tf_op jit(solution)/shard_map/pallas_call | solution.py:344
  46.6 0.7 %copy.9 = bf16[256,512]{1,0:T(8,128)(2,1)} copy(bf16[256,512]{1,0:T(8,128)(2,1)S(1)} %bitcast.1) | data formatting | bytes 524288
Async XLA Ops:
  0.7 1.7 %copy-start = (bf16[1536,768]{1,0:T(8,128)(2,1)S(1)}, bf16[1536,768]{1,0:T(8,128)(2,1)}, u32[]{:S(2)}) copy-start(bf16[1536,768]{1,0:T(8,128)(2,1)} %q_up_hbm.1) | copy-start | bytes 7077892
  2.4 1.0 %copy-start.1 = (bf16[4,128,512]{2,1,0:T(8,128)(2,1)S(1)}, bf16[4,128,512]{2,1,0:T(8,128)(2,1)}, u32[]{:S(2)}) copy-start(bf16[4,128,512]{2,1,0:T(8,128)(2,1)} %absorb_key_hbm.1) | copy-start | bytes 1572868
  3.4 1.0 %copy-start.2 = (bf16[4,512,128]{2,1,0:T(8,128)(2,1)S(1)}, bf16[4,512,128]{2,1,0:T(8,128)(2,1)}, u32[]{:S(2)}) copy-start(bf16[4,512,128]{2,1,0:T(8,128)(2,1)} %absorb_value_hbm.1) | copy-start | bytes 1572868
  4.4 0.9 %copy-start.3 = (bf16[64,1536]{1,0:T(8,128)(2,1)S(1)}, bf16[64,1536]{1,0:T(8,128)(2,1)}, u32[]{:S(2)}) copy-start(bf16[64,1536]{1,0:T(8,128)(2,1)} %query_ref.1) | copy-start | bytes 589828
  5.4 0.9 %copy-start.4 = (bf16[64,576]{1,0:T(8,128)(2,1)S(1)}, bf16[64,576]{1,0:T(8,128)(2,1)}, u32[]{:S(2)}) copy-start(bf16[64,576]{1,0:T(8,128)(2,1)} %kv_ref.1) | copy-start | bytes 221188
  6.3 0.7 %copy-start.5 = (s32[8]{0:T(128)S(1)}, s32[8]{0:T(128)}, u32[]{:S(2)}) copy-start(s32[8]{0:T(128)} %owner_ref.1) | copy-start | bytes 100

commit v2 on v1

--- a/solution.py
+++ b/solution.py
@@ -32,13 +32,15 @@
     ctx_count,
     head_devices,
     owner_ref,
-    query_ref,
-    gain_ref,
-    kv_ref,
+    query_hbm,
+    gain_hbm,
+    kv_hbm,
     q_up_hbm,
     absorb_key_hbm,
     absorb_value_hbm,
     out_ref,
+    query_ref,
+    gain_ref,
     q_up_ref,
     absorb_key_ref,
     absorb_value_ref,
@@ -83,12 +85,24 @@
 
     sibling = other_core(ctx)
 
+    halves = head_devices // 2
+    half_pieces = ctx_count * halves
+
+    def slot_of(origin, piece):
+        return lax.div(piece, halves) * half_pieces + origin * halves + lax.rem(piece, halves)
+
     loads = [
+        pltpu.make_async_copy(kv_hbm, kv_all.at[slot_of(ctx, z)], load_sem.at[3]),
+        pltpu.make_async_copy(query_hbm, query_ref, load_sem.at[4]),
+        pltpu.make_async_copy(gain_hbm, gain_ref, load_sem.at[5]),
         pltpu.make_async_copy(q_up_hbm, q_up_ref, load_sem.at[0]),
         pltpu.make_async_copy(absorb_key_hbm, absorb_key_ref, load_sem.at[1]),
         pltpu.make_async_copy(absorb_value_hbm, absorb_value_ref, load_sem.at[2]),
     ]
 
+    for load in loads:
+        load.start()
+
     barrier = pltpu.get_barrier_semaphore()
     for bit in range(bits):
         pl.semaphore_signal(barrier, inc=1, device_id=(across(1 << bit), z), device_id_type=MESH)
@@ -102,9 +116,7 @@
     def _():
         pl.semaphore_signal(barrier, inc=1, device_id=(ctx, z + 1), device_id_type=MESH)
 
-    for load in loads:
-        load.start()
-    kv_all[ctx * head_devices + z] = kv_ref[...]
+    loads[0].wait()
     pl.semaphore_wait(
         barrier, bits + 1 + jnp.where(z > 0, 1, 0) + jnp.where(z < last, 1, 0)
     )
@@ -112,7 +124,7 @@
     sent = []
 
     def kv_copy(origin, piece, slot, target):
-        index = origin * head_devices + piece
+        index = slot_of(origin, piece)
         return pltpu.make_async_remote_copy(
             src_ref=kv_all.at[index],
             dst_ref=kv_all.at[index],
@@ -191,11 +203,13 @@
                 norm_copy(z + step, False).start()
 
     own_block(0)
+    loads[1].wait()
+    loads[2].wait()
     query_f32 = query_ref[...].astype(jnp.float32)
     normed_all[z] = (
         query_f32
         * lax.rsqrt(jnp.mean(query_f32 * query_f32, axis=-1, keepdims=True) + epsilon)
-        * gain_ref[...].astype(jnp.float32)
+        * gain_ref[...].reshape(1, -1).astype(jnp.float32)
     ).astype(jnp.bfloat16)
 
     def send_norm():
@@ -212,27 +226,33 @@
 
     def tables():
         own = owner_ref[ctx]
-        offset = lax.broadcasted_iota(jnp.int32, (tok_dev, 1), 0)
+        groups = 128 // half_width
+        span = tok_dev // groups
+        lanes = lax.broadcasted_iota(jnp.int32, (span, 128), 1)
+        offset = lax.broadcasted_iota(jnp.int32, (span, 128), 0) + span * lax.div(
+            lanes, half_width
+        )
         places = jnp.where(
             offset < half_len,
             own * half_len + offset,
             (2 * ctx_count - 1 - own) * half_len + offset - half_len,
         )
         frequency = jnp.exp(
-            lax.broadcasted_iota(jnp.int32, (1, half_width), 1).astype(jnp.float32)
+            lax.rem(lanes[:1], half_width).astype(jnp.float32)
             * (-math.log(10000.0) / half_width)
         )
         angles = places.astype(jnp.float32) * frequency
-        cosine_ref[...] = jnp.cos(angles).reshape(cosine_ref.shape)
-        sine_ref[...] = jnp.sin(angles).reshape(sine_ref.shape)
+        cosine, sine = jnp.cos(angles), jnp.sin(angles)
+        for group in range(groups):
+            begin = group * half_width
+            cosine_ref[group * span : (group + 1) * span] = cosine[:, begin : begin + half_width]
+            sine_ref[group * span : (group + 1) * span] = sine[:, begin : begin + half_width]
         lane = lax.broadcasted_iota(jnp.int32, (1, half_len), 1)
         for index in range(ctx_count):
             owner = owner_ref[index]
-            begin = index * tok_dev
-            key_pos_ref[:, begin : begin + half_len] = owner * half_len + lane
-            key_pos_ref[:, begin + half_len : begin + tok_dev] = (
-                2 * ctx_count - 1 - owner
-            ) * half_len + lane
+            columns = slice(index * half_len, (index + 1) * half_len)
+            key_pos_ref[:1, columns] = owner * half_len + lane
+            key_pos_ref[1:, columns] = (2 * ctx_count - 1 - owner) * half_len + lane
 
     distances = [
         [r for r in range(chips) if bin(r).count("1") == level] for level in range(bits + 1)
@@ -248,10 +268,12 @@
                     relay(stage - level, relative)
         if stage == max(last - 1, 0):
             tables()
-            for load in loads:
+            for load in loads[3:]:
                 load.wait()
         if stage == last and last > 0:
             norm_step(1)
+    if last > 1:
+        norm_step(2)
 
     for relative in range(chips):
         for piece in range(head_devices):
@@ -267,8 +289,8 @@
         projected_ref[...] = jnp.dot(
             normed_all[block], q_up_ref[...], preferred_element_type=jnp.float32
         )
-        cosine = cosine_ref[block]
-        sine = sine_ref[block]
+        cosine = cosine_ref[pl.ds(pl.multiple_of(block * rows, rows), rows)]
+        sine = sine_ref[pl.ds(pl.multiple_of(block * rows, rows), rows)]
         for head in range(head_count):
             begin = head * head_width
             q_nope = projected_ref[:, begin : begin + nope_width].astype(jnp.bfloat16)
@@ -282,7 +304,7 @@
                 [front * cosine - back * sine, front * sine + back * cosine], axis=-1
             ).astype(jnp.bfloat16)
 
-        @pl.when(step + 2 <= last)
+        @pl.when(jnp.logical_and(step > 0, step + 2 <= last))
         def _():
             norm_step(step + 2)
 
@@ -291,23 +313,43 @@
         query_pos = base + lax.rem(
             lax.broadcasted_iota(jnp.int32, (head_count * rows, 1), 0), rows
         )
-        keys = kv_all[...].reshape(ctx_count * tok_dev, latent_width + rope_width)
-        scores = lax.dot_general(
-            queries_ref[...], keys, (((1,), (1,)), ((), ())), preferred_element_type=jnp.float32
-        )
-        scores = jnp.where(key_pos_ref[...] <= query_pos, scores, masked_score)
-        peak = jnp.max(scores, axis=-1, keepdims=True)
-        weights = jnp.exp2((scores - peak) * factor)
-        total = jnp.sum(weights, axis=-1, keepdims=True)
-        weighted = jnp.dot(
-            weights.astype(jnp.bfloat16),
-            keys[:, :latent_width],
-            preferred_element_type=jnp.float32,
-        )
-        latent_out = (weighted / total).astype(jnp.bfloat16)
+
+        def attend(upper):
+            def rows_of(half):
+                return kv_all[half * half_pieces : (half + 1) * half_pieces].reshape(
+                    ctx_count * half_len, latent_width + rope_width
+                )
+
+            def score(keys):
+                return lax.dot_general(
+                    queries_ref[...],
+                    keys,
+                    (((1,), (1,)), ((), ())),
+                    preferred_element_type=jnp.float32,
+                )
+
+            allowed = key_pos_ref[int(upper) : int(upper) + 1] <= query_pos
+            parts = [jnp.where(allowed, score(rows_of(int(upper))), masked_score)]
+            peak = jnp.max(parts[0], axis=-1, keepdims=True)
+            if upper:
+                parts.append(score(rows_of(0)))
+                peak = jnp.maximum(peak, jnp.max(parts[1], axis=-1, keepdims=True))
+            total, weighted = 0.0, 0.0
+            for half, part in zip((int(upper), 0), parts):
+                weights = jnp.exp2((part - peak) * factor)
+                total += jnp.sum(weights, axis=-1, keepdims=True)
+                weighted += jnp.dot(
+                    weights.astype(jnp.bfloat16),
+                    rows_of(half)[:, :latent_width],
+                    preferred_element_type=jnp.float32,
+                )
+            queries_ref[:, :latent_width] = (weighted / total).astype(jnp.bfloat16)
+
+        pl.when(block < halves)(functools.partial(attend, False))
+        pl.when(block >= halves)(functools.partial(attend, True))
         for head in range(head_count):
             out_ref[block, :, head * value_width : (head + 1) * value_width] = jnp.dot(
-                latent_out[head * rows : (head + 1) * rows],
+                queries_ref[head * rows : (head + 1) * rows, :latent_width],
                 absorb_value_ref[head],
                 preferred_element_type=jnp.float32,
             ).astype(jnp.bfloat16)
@@ -344,17 +386,19 @@
     out = pl.pallas_call(
         functools.partial(kernel, ctx_count, head_devices),
         out_shape=jax.ShapeDtypeStruct((head_devices, rows, head_count * value_width), bf16),
-        in_specs=[pl.BlockSpec(memory_space=pltpu.SMEM), whole, whole, whole, away, away, away],
+        in_specs=[pl.BlockSpec(memory_space=pltpu.SMEM)] + [away] * 6,
         out_specs=whole,
         scratch_shapes=[
+            pltpu.VMEM(query_latent.shape, bf16),
+            pltpu.VMEM(norm_gain.shape, bf16),
             pltpu.VMEM(q_up.shape, bf16),
             pltpu.VMEM(absorb_key.shape, bf16),
             pltpu.VMEM(absorb_value.shape, bf16),
             pltpu.VMEM((piece_count, rows, kv_width), bf16),
             pltpu.VMEM((head_devices, rows, query_width), bf16),
-            pltpu.VMEM((head_devices, rows, rope_half), f32),
-            pltpu.VMEM((head_devices, rows, rope_half), f32),
-            pltpu.VMEM((1, ctx_count * tok_dev), jnp.int32),
+            pltpu.VMEM((tok_dev, rope_half), f32),
+            pltpu.VMEM((tok_dev, rope_half), f32),
+            pltpu.VMEM((2, ctx_count * tok_dev // 2), jnp.int32),
             pltpu.VMEM((rows, q_up.shape[1]), f32),
             pltpu.VMEM((head_count * rows, kv_width), bf16),
             pltpu.SemaphoreType.DMA((piece_count,)),
@@ -362,15 +406,15 @@
             pltpu.SemaphoreType.DMA((head_devices,)),
             pltpu.SemaphoreType.DMA((head_devices,)),
             pltpu.SemaphoreType.DMA((head_devices,)),
-            pltpu.SemaphoreType.DMA((3,)),
+            pltpu.SemaphoreType.DMA((6,)),
         ],
         compiler_params=pltpu.CompilerParams(
-            collective_id=0, has_side_effects=True, vmem_limit_bytes=48 * 1024 * 1024
+            collective_id=0, has_side_effects=True, vmem_limit_bytes=60 * 1024 * 1024
         ),
     )(
         block_owner,
         query_latent,
-        norm_gain.reshape(1, query_width),
+        norm_gain,
         kv_latent,
         q_up,
         absorb_key,

time: 47.7 us -> 40.4 us (0.85)
  the two profiles are of different devices: /device:TPU:1 before, /device:TPU:0 now
where the time goes in v2:
time: 40.4 us; the launch traced here: 39.9 us
  Pallas kernels  38.2 us (95%)
  local copies, waits for them, and re-layouts  1.67 us (4%)
    pallas_call x1, Pallas kernels, per_device(): pl.pallas_call(functools.partial(kernel, ctx_count, head_devices), out_sh...  38.2 us
    unnamed x1, local copies, waits for them, and re-layouts  1.67 us

profile of v2, /device:TPU:0, one launch (start us, length us, event | category | flops | bytes accessed | tf_op | source)
XLA Modules:
  0.0 39.9 jit_solution(13162535890885931513)
XLA Ops:
  0.0 38.2 %shard_map.73 = bf16[4,64,512]{2,1,0:T(8,128)(2,1)} custom-call(s32[8]{0:T(128)} %owner_ref.1, bf16[64,1536]{1,0:T(8,128)(2,1)} %query_hbm.1, bf16[1536]{0:T(1024)(128)(2,1)} %gain_hbm.1, bf16[64,576]{1,0:T(8,128)(2,1)} %kv_hbm.1, bf16[1536,768]{1,0:T(8,128)(2,1)} %q_up_hbm.1, bf16[4,128,512]{2,1,0:T(8,128)(2,1)} %absorb_key_hbm.1, ...), custom_call_target="tpu_custom_call" | custom-call | tf_op jit(solution)/shard_map/pallas_call | solution.py:386
  38.2 1.7 %copy.9 = bf16[256,512]{1,0:T(8,128)(2,1)} copy(bf16[256,512]{1,0:T(8,128)(2,1)} %bitcast.1) | data formatting | bytes 524288

commit v3 on v2

--- a/solution.py
+++ b/solution.py
@@ -108,18 +108,25 @@
         pl.semaphore_signal(barrier, inc=1, device_id=(across(1 << bit), z), device_id_type=MESH)
     pl.semaphore_signal(barrier, inc=1, device_id=(sibling, z), device_id_type=MESH)
 
-    @pl.when(z > 0)
-    def _():
-        pl.semaphore_signal(barrier, inc=1, device_id=(ctx, z - 1), device_id_type=MESH)
-
-    @pl.when(z < last)
-    def _():
-        pl.semaphore_signal(barrier, inc=1, device_id=(ctx, z + 1), device_id_type=MESH)
+    kv_reach = min(3, last)
+    norm_reach = min(2, last)
+    partners = bits + 1
+    for step in range(1, kv_reach + 1):
+        for valid, place in ((z + step <= last, z + step), (z >= step, z - step)):
+            partners = partners + jnp.where(valid, 1, 0)
+            when(
+                valid,
+                functools.partial(
+                    pl.semaphore_signal,
+                    barrier,
+                    inc=1,
+                    device_id=(ctx, place),
+                    device_id_type=MESH,
+                ),
+            )
 
     loads[0].wait()
-    pl.semaphore_wait(
-        barrier, bits + 1 + jnp.where(z > 0, 1, 0) + jnp.where(z < last, 1, 0)
-    )
+    pl.semaphore_wait(barrier, partners)
 
     sent = []
 
@@ -148,13 +155,16 @@
         return [(z >= step, z - step, 1), (z + step <= last, z + step, -1)]
 
     def own_block(step):
+        if step == 0:
+            for far in range(1, kv_reach + 1):
+                send_kv(z + far <= last, ctx, z, (ctx, z + far))
+                send_kv(z >= far, ctx, z, (ctx, z - far))
         for valid, piece, way in pieces(step):
             if step > 0:
                 wait_kv(valid, ctx, piece)
-            if way >= 0 and step < last:
-                send_kv(both(valid, z < last), ctx, piece, (ctx, z + 1))
-            if way <= 0 and step < last:
-                send_kv(both(valid, z > 0), ctx, piece, (ctx, z - 1))
+            if kv_reach <= step < last:
+                onward = z < last if way > 0 else z > 0
+                send_kv(both(valid, onward), ctx, piece, (ctx, z + way))
             for bit in range(bits):
                 send_kv(valid, ctx, piece, (across(1 << bit), z))
             send_kv(valid, ctx, piece, (sibling, z))
@@ -172,35 +182,25 @@
                     send_kv(both(valid, odd), origin, piece, (across(1 << bit), z))
             send_kv(valid, origin, piece, (sibling, z))
 
-    def norm_copy(block, upward):
-        send_sem, target = (
-            (norm_send_up, z + 1) if upward else (norm_send_down, z - 1)
-        )
+    def norm_copy(block, way, far=1):
+        send_sem = norm_send_up if way > 0 else norm_send_down
         return pltpu.make_async_remote_copy(
             src_ref=normed_all.at[block],
             dst_ref=normed_all.at[block],
-            send_sem=send_sem.at[block],
+            send_sem=send_sem.at[block if far == 1 else last + far],
             recv_sem=norm_recv.at[block],
-            device_id=(ctx, target),
+            device_id=(ctx, z + far * way),
             device_id_type=MESH,
         )
 
     def norm_step(step):
-        @pl.when(z >= step)
-        def _():
-            norm_copy(z - step, True).wait_recv()
-
-            @pl.when(z < last)
-            def _():
-                norm_copy(z - step, True).start()
-
-        @pl.when(z + step <= last)
-        def _():
-            norm_copy(z + step, False).wait_recv()
-
-            @pl.when(z > 0)
-            def _():
-                norm_copy(z + step, False).start()
+        for valid, block, way, onward in (
+            (z >= step, z - step, 1, z < last),
+            (z + step <= last, z + step, -1, z > 0),
+        ):
+            copy = norm_copy(block, way)
+            when(valid, copy.wait_recv)
+            when(both(valid, jnp.logical_and(onward, step >= norm_reach)), copy.start)
 
     own_block(0)
     loads[1].wait()
@@ -212,14 +212,9 @@
         * gain_ref[...].reshape(1, -1).astype(jnp.float32)
     ).astype(jnp.bfloat16)
 
-    def send_norm():
-        @pl.when(z < last)
-        def _():
-            norm_copy(z, True).start()
-
-        @pl.when(z > 0)
-        def _():
-            norm_copy(z, False).start()
+    for far in range(1, norm_reach + 1):
+        when(z + far <= last, norm_copy(z, 1, far).start)
+        when(z >= far, norm_copy(z, -1, far).start)
 
     def half_base(owner, upper):
         return jnp.where(upper, 2 * ctx_count - 1 - owner, owner) * half_len
@@ -260,32 +255,26 @@
     for stage in range(head_devices + bits):
         if 0 < stage < head_devices:
             own_block(stage)
-        if stage == max(last - 1, 0):
-            send_norm()
         for level in range(1, bits + 1):
             if 0 <= stage - level < head_devices:
                 for relative in distances[level]:
                     relay(stage - level, relative)
-        if stage == max(last - 1, 0):
+        if stage == 0:
             tables()
-            for load in loads[3:]:
-                load.wait()
-        if stage == last and last > 0:
-            norm_step(1)
-    if last > 1:
-        norm_step(2)
-
-    for relative in range(chips):
-        for piece in range(head_devices):
-            wait_kv(True, other_core(across(relative)), piece)
+    for step in range(1, norm_reach + 1):
+        norm_step(step)
+    for load in loads[3:]:
+        load.wait()
 
     factor = float(head_width) ** (-0.5) * math.log2(math.e)
     shorter = jnp.minimum(z, last - z)
 
-    def block_body(step, carry):
+    def block_at(step):
         near = z + lax.div(step + 1, 2) * (1 - 2 * lax.rem(step, 2))
         far = jnp.where(z > last - z, last - step, step)
-        block = jnp.where(step <= 2 * shorter, near, far)
+        return jnp.where(step <= 2 * shorter, near, far)
+
+    def project(block):
         projected_ref[...] = jnp.dot(
             normed_all[block], q_up_ref[...], preferred_element_type=jnp.float32
         )
@@ -304,10 +293,13 @@
                 [front * cosine - back * sine, front * sine + back * cosine], axis=-1
             ).astype(jnp.bfloat16)
 
-        @pl.when(jnp.logical_and(step > 0, step + 2 <= last))
-        def _():
-            norm_step(step + 2)
-
+    project(z)
+    for relative in range(chips):
+        for piece in range(head_devices):
+            wait_kv(True, other_core(across(relative)), piece)
+
+    def block_body(step, carry):
+        block = block_at(step)
         offset = block * rows
         base = half_base(owner_ref[ctx], offset >= half_len) + lax.rem(offset, half_len)
         query_pos = base + lax.rem(
@@ -353,20 +345,27 @@
                 absorb_value_ref[head],
                 preferred_element_type=jnp.float32,
             ).astype(jnp.bfloat16)
+
+        @pl.when(step < last)
+        def _():
+            @pl.when(step + 1 > norm_reach)
+            def _():
+                norm_step(step + 1)
+
+            project(block_at(step + 1))
+
         return carry
 
     lax.fori_loop(0, head_devices, block_body, 0)
 
     for condition, copy in sent:
         when(condition, copy.wait_send)
-    for block in range(head_devices):
-        @pl.when(jnp.logical_and(z >= block, z < last))
-        def _():
-            norm_copy(block, True).wait_send()
-
-        @pl.when(jnp.logical_and(z <= block, z > 0))
-        def _():
-            norm_copy(block, False).wait_send()
+    for far in range(1, norm_reach + 1):
+        when(z + far <= last, norm_copy(z, 1, far).wait_send)
+        when(z >= far, norm_copy(z, -1, far).wait_send)
+    for step in range(norm_reach, last):
+        when(both(z >= step, z < last), norm_copy(z - step, 1).wait_send)
+        when(both(z + step <= last, z > 0), norm_copy(z + step, -1).wait_send)
 
 
 def per_device(query_latent, norm_gain, kv_latent, q_up, absorb_key, absorb_value, block_owner):
@@ -379,7 +378,7 @@
     tok_dev = rows * head_devices
     piece_count = ctx_count * head_devices
     bits = (ctx_count // 2).bit_length() - 1
-    slots = head_devices * ((ctx_count // 2) * (bits + 1) * 2 + 4)
+    slots = head_devices * ((ctx_count // 2) * (bits + 1) * 2 + 8)
     bf16, f32 = jnp.bfloat16, jnp.float32
     whole = pl.BlockSpec(memory_space=pltpu.VMEM)
     away = pl.BlockSpec(memory_space=pl.ANY)
@@ -404,8 +403,8 @@
             pltpu.SemaphoreType.DMA((piece_count,)),
             pltpu.SemaphoreType.DMA((slots,)),
             pltpu.SemaphoreType.DMA((head_devices,)),
-            pltpu.SemaphoreType.DMA((head_devices,)),
-            pltpu.SemaphoreType.DMA((head_devices,)),
+            pltpu.SemaphoreType.DMA((head_devices + 2,)),
+            pltpu.SemaphoreType.DMA((head_devices + 2,)),
             pltpu.SemaphoreType.DMA((6,)),
         ],
         compiler_params=pltpu.CompilerParams(

time: 40.4 us -> 42.3 us (1.047)
  Pallas kernels: 38.2 us -> 40.5 us
    pallas_call x1, Pallas kernels: 38.2 us -> 40.5 us  [per_device(): pl.pallas_call(functools.partial(kernel, ctx_count, head_devices), out_sh...]
where the time goes in v3:
time: 42.3 us; the launch traced here: 42.1 us
  Pallas kernels  40.5 us (96%)
  local copies, waits for them, and re-layouts  1.67 us (4%)
    pallas_call x1, Pallas kernels, per_device(): pl.pallas_call(functools.partial(kernel, ctx_count, head_devices), out_sh...  40.5 us
    unnamed x1, local copies, waits for them, and re-layouts  1.67 us

profile of v3, /device:TPU:0, one launch (start us, length us, event | category | flops | bytes accessed | tf_op | source)
XLA Modules:
  0.0 42.1 jit_solution(6663507745889416408)
XLA Ops:
  0.0 40.5 %shard_map.73 = bf16[4,64,512]{2,1,0:T(8,128)(2,1)} custom-call(s32[8]{0:T(128)} %owner_ref.1, bf16[64,1536]{1,0:T(8,128)(2,1)} %query_hbm.1, bf16[1536]{0:T(1024)(128)(2,1)} %gain_hbm.1, bf16[64,576]{1,0:T(8,128)(2,1)} %kv_hbm.1, bf16[1536,768]{1,0:T(8,128)(2,1)} %q_up_hbm.1, bf16[4,128,512]{2,1,0:T(8,128)(2,1)} %absorb_key_hbm.1, ...), custom_call_target="tpu_custom_call" | custom-call | tf_op jit(solution)/shard_map/pallas_call | solution.py:385
  40.5 1.7 %copy.9 = bf16[256,512]{1,0:T(8,128)(2,1)} copy(bf16[256,512]{1,0:T(8,128)(2,1)} %bitcast.1) | data formatting | bytes 524288

commit v4 on v3

--- a/solution.py
+++ b/solution.py
@@ -39,6 +39,7 @@
     absorb_key_hbm,
     absorb_value_hbm,
     out_ref,
+    kv_ref,
     query_ref,
     gain_ref,
     q_up_ref,
@@ -92,7 +93,7 @@
         return lax.div(piece, halves) * half_pieces + origin * halves + lax.rem(piece, halves)
 
     loads = [
-        pltpu.make_async_copy(kv_hbm, kv_all.at[slot_of(ctx, z)], load_sem.at[3]),
+        pltpu.make_async_copy(kv_hbm, kv_ref, load_sem.at[3]),
         pltpu.make_async_copy(query_hbm, query_ref, load_sem.at[4]),
         pltpu.make_async_copy(gain_hbm, gain_ref, load_sem.at[5]),
         pltpu.make_async_copy(q_up_hbm, q_up_ref, load_sem.at[0]),
@@ -126,6 +127,13 @@
             )
 
     loads[0].wait()
+    kv_width = latent_width + rope_width
+    own_slot = slot_of(ctx, z)
+    kv_all[own_slot, :, :kv_width] = kv_ref[...]
+    padding = kv_all.shape[2] - kv_width
+    if padding:
+        kv_all[own_slot, :, kv_width:] = jnp.zeros((rows, padding), jnp.bfloat16)
+        queries_ref[:, kv_width:] = jnp.zeros((head_count * rows, padding), jnp.bfloat16)
     pl.semaphore_wait(barrier, partners)
 
     sent = []
@@ -289,7 +297,7 @@
             back = projected_ref[:, begin + half_width : begin + rope_width]
             span = slice(head * rows, (head + 1) * rows)
             queries_ref[span, :latent_width] = q_abs.astype(jnp.bfloat16)
-            queries_ref[span, latent_width:] = jnp.concatenate(
+            queries_ref[span, latent_width:kv_width] = jnp.concatenate(
                 [front * cosine - back * sine, front * sine + back * cosine], axis=-1
             ).astype(jnp.bfloat16)
 
@@ -309,7 +317,7 @@
         def attend(upper):
             def rows_of(half):
                 return kv_all[half * half_pieces : (half + 1) * half_pieces].reshape(
-                    ctx_count * half_len, latent_width + rope_width
+                    ctx_count * half_len, kv_all.shape[2]
                 )
 
             def score(keys):
@@ -374,6 +382,7 @@
     rows, query_width = query_latent.shape
     kv_width = kv_latent.shape[1]
     head_count, _, value_width = absorb_value.shape
+    padded_width = 128 * pl.cdiv(kv_width, 128)
     rope_half = (kv_width - absorb_key.shape[2]) // 2
     tok_dev = rows * head_devices
     piece_count = ctx_count * head_devices
@@ -388,18 +397,19 @@
         in_specs=[pl.BlockSpec(memory_space=pltpu.SMEM)] + [away] * 6,
         out_specs=whole,
         scratch_shapes=[
+            pltpu.VMEM(kv_latent.shape, bf16),
             pltpu.VMEM(query_latent.shape, bf16),
             pltpu.VMEM(norm_gain.shape, bf16),
             pltpu.VMEM(q_up.shape, bf16),
             pltpu.VMEM(absorb_key.shape, bf16),
             pltpu.VMEM(absorb_value.shape, bf16),
-            pltpu.VMEM((piece_count, rows, kv_width), bf16),
+            pltpu.VMEM((piece_count, rows, padded_width), bf16),
             pltpu.VMEM((head_devices, rows, query_width), bf16),
             pltpu.VMEM((tok_dev, rope_half), f32),
             pltpu.VMEM((tok_dev, rope_half), f32),
             pltpu.VMEM((2, ctx_count * tok_dev // 2), jnp.int32),
             pltpu.VMEM((rows, q_up.shape[1]), f32),
-            pltpu.VMEM((head_count * rows, kv_width), bf16),
+            pltpu.VMEM((head_count * rows, padded_width), bf16),
             pltpu.SemaphoreType.DMA((piece_count,)),
             pltpu.SemaphoreType.DMA((slots,)),
             pltpu.SemaphoreType.DMA((head_devices,)),

time: 42.3 us -> 42.3 us (level)
  no operation moved by 1% of the time
where the time goes in v4:
time: 42.3 us; the launch traced here: 42.1 us
  Pallas kernels  40.5 us (96%)
  local copies, waits for them, and re-layouts  1.67 us (4%)
    pallas_call x1, Pallas kernels, per_device(): pl.pallas_call(functools.partial(kernel, ctx_count, head_devices), out_sh...  40.5 us
    unnamed x1, local copies, waits for them, and re-layouts  1.67 us

profile of v4, /device:TPU:0, one launch (start us, length us, event | category | flops | bytes accessed | tf_op | source)
XLA Modules:
  0.0 42.1 jit_solution(18195721861331113491)
XLA Ops:
  0.0 40.5 %shard_map.73 = bf16[4,64,512]{2,1,0:T(8,128)(2,1)} custom-call(s32[8]{0:T(128)} %owner_ref.1, bf16[64,1536]{1,0:T(8,128)(2,1)} %query_hbm.1, bf16[1536]{0:T(1024)(128)(2,1)} %gain_hbm.1, bf16[64,576]{1,0:T(8,128)(2,1)} %kv_hbm.1, bf16[1536,768]{1,0:T(8,128)(2,1)} %q_up_hbm.1, bf16[4,128,512]{2,1,0:T(8,128)(2,1)} %absorb_key_hbm.1, ...), custom_call_target="tpu_custom_call" | custom-call | tf_op jit(solution)/shard_map/pallas_call | solution.py:394
  40.5 1.7 %copy.9 = bf16[256,512]{1,0:T(8,128)(2,1)} copy(bf16[256,512]{1,0:T(8,128)(2,1)} %bitcast.1) | data formatting | bytes 524288

commit v5 on v3

--- a/solution.py
+++ b/solution.py
@@ -108,8 +108,8 @@
         pl.semaphore_signal(barrier, inc=1, device_id=(across(1 << bit), z), device_id_type=MESH)
     pl.semaphore_signal(barrier, inc=1, device_id=(sibling, z), device_id_type=MESH)
 
-    kv_reach = min(3, last)
-    norm_reach = min(2, last)
+    kv_reach = min(2, last)
+    norm_reach = min(1, last)
     partners = bits + 1
     for step in range(1, kv_reach + 1):
         for valid, place in ((z + step <= last, z + step), (z >= step, z - step)):
@@ -346,11 +346,16 @@
                 preferred_element_type=jnp.float32,
             ).astype(jnp.bfloat16)
 
+        @pl.when(step + 2 < last)
+        def _():
+            norm_step(step + 2)
+
         @pl.when(step < last)
         def _():
-            @pl.when(step + 1 > norm_reach)
-            def _():
-                norm_step(step + 1)
+            if last > 1:
+                @pl.when(step + 1 == last)
+                def _():
+                    norm_step(last)
 
             project(block_at(step + 1))
 

time: 42.3 us -> 40.2 us (0.950)
  Pallas kernels: 40.5 us -> 38.3 us
    pallas_call x1, Pallas kernels: 40.5 us -> 38.3 us  [per_device(): pl.pallas_call(functools.partial(kernel, ctx_count, head_devices), out_sh...]
where the time goes in v5:
time: 40.2 us; the launch traced here: 40 us
  Pallas kernels  38.3 us (95%)
  local copies, waits for them, and re-layouts  1.67 us (4%)
    pallas_call x1, Pallas kernels, per_device(): pl.pallas_call(functools.partial(kernel, ctx_count, head_devices), out_sh...  38.3 us
    unnamed x1, local copies, waits for them, and re-layouts  1.67 us

profile of v5, /device:TPU:0, one launch (start us, length us, event | category | flops | bytes accessed | tf_op | source)
XLA Modules:
  0.0 40.0 jit_solution(7589024409211328706)
XLA Ops:
  0.0 38.3 %shard_map.73 = bf16[4,64,512]{2,1,0:T(8,128)(2,1)} custom-call(s32[8]{0:T(128)} %owner_ref.1, bf16[64,1536]{1,0:T(8,128)(2,1)} %query_hbm.1, bf16[1536]{0:T(1024)(128)(2,1)} %gain_hbm.1, bf16[64,576]{1,0:T(8,128)(2,1)} %kv_hbm.1, bf16[1536,768]{1,0:T(8,128)(2,1)} %q_up_hbm.1, bf16[4,128,512]{2,1,0:T(8,128)(2,1)} %absorb_key_hbm.1, ...), custom_call_target="tpu_custom_call" | custom-call | tf_op jit(solution)/shard_map/pallas_call | solution.py:390
  38.4 1.7 %copy.9 = bf16[256,512]{1,0:T(8,128)(2,1)} copy(bf16[256,512]{1,0:T(8,128)(2,1)} %bitcast.1) | data formatting | bytes 524288

commit v6 on v3

--- a/solution.py
+++ b/solution.py
@@ -108,8 +108,8 @@
         pl.semaphore_signal(barrier, inc=1, device_id=(across(1 << bit), z), device_id_type=MESH)
     pl.semaphore_signal(barrier, inc=1, device_id=(sibling, z), device_id_type=MESH)
 
-    kv_reach = min(3, last)
-    norm_reach = min(2, last)
+    kv_reach = min(2, last)
+    norm_reach = min(1, last)
     partners = bits + 1
     for step in range(1, kv_reach + 1):
         for valid, place in ((z + step <= last, z + step), (z >= step, z - step)):
@@ -182,11 +182,15 @@
                     send_kv(both(valid, odd), origin, piece, (across(1 << bit), z))
             send_kv(valid, origin, piece, (sibling, z))
 
+    def normed_at(block):
+        begin = pl.multiple_of(lax.rem(block, 2) * rows, rows)
+        return normed_all.at[lax.div(block, 2), pl.ds(begin, rows)]
+
     def norm_copy(block, way, far=1):
         send_sem = norm_send_up if way > 0 else norm_send_down
         return pltpu.make_async_remote_copy(
-            src_ref=normed_all.at[block],
-            dst_ref=normed_all.at[block],
+            src_ref=normed_at(block),
+            dst_ref=normed_at(block),
             send_sem=send_sem.at[block if far == 1 else last + far],
             recv_sem=norm_recv.at[block],
             device_id=(ctx, z + far * way),
@@ -206,7 +210,7 @@
     loads[1].wait()
     loads[2].wait()
     query_f32 = query_ref[...].astype(jnp.float32)
-    normed_all[z] = (
+    normed_at(z)[...] = (
         query_f32
         * lax.rsqrt(jnp.mean(query_f32 * query_f32, axis=-1, keepdims=True) + epsilon)
         * gain_ref[...].reshape(1, -1).astype(jnp.float32)
@@ -261,25 +265,27 @@
                     relay(stage - level, relative)
         if stage == 0:
             tables()
-    for step in range(1, norm_reach + 1):
-        norm_step(step)
+    norm_step(1)
     for load in loads[3:]:
         load.wait()
 
     factor = float(head_width) ** (-0.5) * math.log2(math.e)
-    shorter = jnp.minimum(z, last - z)
-
-    def block_at(step):
-        near = z + lax.div(step + 1, 2) * (1 - 2 * lax.rem(step, 2))
-        far = jnp.where(z > last - z, last - step, step)
+    pair_rows = 2 * rows
+    own_pair = lax.div(z, 2)
+    last_pair = last // 2
+    shorter = jnp.minimum(own_pair, last_pair - own_pair)
+
+    def pair_at(step):
+        near = own_pair + lax.div(step + 1, 2) * (1 - 2 * lax.rem(step, 2))
+        far = jnp.where(own_pair > last_pair - own_pair, last_pair - step, step)
         return jnp.where(step <= 2 * shorter, near, far)
 
-    def project(block):
+    def project(pair):
         projected_ref[...] = jnp.dot(
-            normed_all[block], q_up_ref[...], preferred_element_type=jnp.float32
-        )
-        cosine = cosine_ref[pl.ds(pl.multiple_of(block * rows, rows), rows)]
-        sine = sine_ref[pl.ds(pl.multiple_of(block * rows, rows), rows)]
+            normed_all[pair], q_up_ref[...], preferred_element_type=jnp.float32
+        )
+        cosine = cosine_ref[pl.ds(pl.multiple_of(pair * pair_rows, pair_rows), pair_rows)]
+        sine = sine_ref[pl.ds(pl.multiple_of(pair * pair_rows, pair_rows), pair_rows)]
         for head in range(head_count):
             begin = head * head_width
             q_nope = projected_ref[:, begin : begin + nope_width].astype(jnp.bfloat16)
@@ -287,23 +293,26 @@
             begin += nope_width
             front = projected_ref[:, begin : begin + half_width]
             back = projected_ref[:, begin + half_width : begin + rope_width]
-            span = slice(head * rows, (head + 1) * rows)
+            span = slice(head * pair_rows, (head + 1) * pair_rows)
             queries_ref[span, :latent_width] = q_abs.astype(jnp.bfloat16)
             queries_ref[span, latent_width:] = jnp.concatenate(
                 [front * cosine - back * sine, front * sine + back * cosine], axis=-1
             ).astype(jnp.bfloat16)
 
-    project(z)
+    project(own_pair)
     for relative in range(chips):
         for piece in range(head_devices):
             wait_kv(True, other_core(across(relative)), piece)
 
-    def block_body(step, carry):
-        block = block_at(step)
-        offset = block * rows
+    if last > 1:
+        norm_step(2)
+
+    def pair_body(step, carry):
+        pair = pair_at(step)
+        offset = pair * pair_rows
         base = half_base(owner_ref[ctx], offset >= half_len) + lax.rem(offset, half_len)
         query_pos = base + lax.rem(
-            lax.broadcasted_iota(jnp.int32, (head_count * rows, 1), 0), rows
+            lax.broadcasted_iota(jnp.int32, (head_count * pair_rows, 1), 0), pair_rows
         )
 
         def attend(upper):
@@ -337,26 +346,28 @@
                 )
             queries_ref[:, :latent_width] = (weighted / total).astype(jnp.bfloat16)
 
-        pl.when(block < halves)(functools.partial(attend, False))
-        pl.when(block >= halves)(functools.partial(attend, True))
+        pl.when(2 * pair < halves)(functools.partial(attend, False))
+        pl.when(2 * pair >= halves)(functools.partial(attend, True))
         for head in range(head_count):
-            out_ref[block, :, head * value_width : (head + 1) * value_width] = jnp.dot(
-                queries_ref[head * rows : (head + 1) * rows, :latent_width],
+            out_ref[pair, :, head * value_width : (head + 1) * value_width] = jnp.dot(
+                queries_ref[head * pair_rows : (head + 1) * pair_rows, :latent_width],
                 absorb_value_ref[head],
                 preferred_element_type=jnp.float32,
             ).astype(jnp.bfloat16)
 
-        @pl.when(step < last)
+        @pl.when(step < last_pair)
         def _():
-            @pl.when(step + 1 > norm_reach)
+            norm_step(2 * step + 3)
+
+            @pl.when(2 * step + 4 <= last)
             def _():
-                norm_step(step + 1)
-
-            project(block_at(step + 1))
+                norm_step(2 * step + 4)
+
+            project(pair_at(step + 1))
 
         return carry
 
-    lax.fori_loop(0, head_devices, block_body, 0)
+    lax.fori_loop(0, head_devices // 2, pair_body, 0)
 
     for condition, copy in sent:
         when(condition, copy.wait_send)
@@ -384,7 +395,7 @@
     away = pl.BlockSpec(memory_space=pl.ANY)
     out = pl.pallas_call(
         functools.partial(kernel, ctx_count, head_devices),
-        out_shape=jax.ShapeDtypeStruct((head_devices, rows, head_count * value_width), bf16),
+        out_shape=jax.ShapeDtypeStruct((head_devices // 2, 2 * rows, head_count * value_width), bf16),
         in_specs=[pl.BlockSpec(memory_space=pltpu.SMEM)] + [away] * 6,
         out_specs=whole,
         scratch_shapes=[
@@ -394,12 +405,12 @@
             pltpu.VMEM(absorb_key.shape, bf16),
             pltpu.VMEM(absorb_value.shape, bf16),
             pltpu.VMEM((piece_count, rows, kv_width), bf16),
-            pltpu.VMEM((head_devices, rows, query_width), bf16),
+            pltpu.VMEM((head_devices // 2, 2 * rows, query_width), bf16),
             pltpu.VMEM((tok_dev, rope_half), f32),
             pltpu.VMEM((tok_dev, rope_half), f32),
             pltpu.VMEM((2, ctx_count * tok_dev // 2), jnp.int32),
-            pltpu.VMEM((rows, q_up.shape[1]), f32),
-            pltpu.VMEM((head_count * rows, kv_width), bf16),
+            pltpu.VMEM((2 * rows, q_up.shape[1]), f32),
+            pltpu.VMEM((2 * head_count * rows, kv_width), bf16),
             pltpu.SemaphoreType.DMA((piece_count,)),
             pltpu.SemaphoreType.DMA((slots,)),
             pltpu.SemaphoreType.DMA((head_devices,)),

time: 42.3 us -> 40.5 us (0.957)
  Pallas kernels: 40.5 us -> 38.7 us
    pallas_call x1, Pallas kernels: 40.5 us -> 38.7 us  [per_device(): pl.pallas_call(functools.partial(kernel, ctx_count, head_devices), out_sh...]
where the time goes in v6:
time: 40.5 us; the launch traced here: 40.4 us
  Pallas kernels  38.7 us (96%)
  local copies, waits for them, and re-layouts  1.67 us (4%)
    pallas_call x1, Pallas kernels, per_device(): pl.pallas_call(functools.partial(kernel, ctx_count, head_devices), out_sh...  38.7 us
    unnamed x1, local copies, waits for them, and re-layouts  1.67 us

profile of v6, /device:TPU:0, one launch (start us, length us, event | category | flops | bytes accessed | tf_op | source)
XLA Modules:
  0.0 40.4 jit_solution(18078287419958200003)
XLA Ops:
  0.0 38.7 %shard_map.73 = bf16[2,128,512]{2,1,0:T(8,128)(2,1)} custom-call(s32[8]{0:T(128)} %owner_ref.1, bf16[64,1536]{1,0:T(8,128)(2,1)} %query_hbm.1, bf16[1536]{0:T(1024)(128)(2,1)} %gain_hbm.1, bf16[64,576]{1,0:T(8,128)(2,1)} %kv_hbm.1, bf16[1536,768]{1,0:T(8,128)(2,1)} %q_up_hbm.1, bf16[4,128,512]{2,1,0:T(8,128)(2,1)} %absorb_key_hbm.1, ...), custom_call_target="tpu_custom_call" | custom-call | tf_op jit(solution)/shard_map/pallas_call | solution.py:396
  38.7 1.7 %copy.9 = bf16[256,512]{1,0:T(8,128)(2,1)} copy(bf16[256,512]{1,0:T(8,128)(2,1)} %bitcast.1) | data formatting | bytes 524288

commit v7 on v6

--- a/solution.py
+++ b/solution.py
@@ -109,7 +109,6 @@
     pl.semaphore_signal(barrier, inc=1, device_id=(sibling, z), device_id_type=MESH)
 
     kv_reach = min(2, last)
-    norm_reach = min(1, last)
     partners = bits + 1
     for step in range(1, kv_reach + 1):
         for valid, place in ((z + step <= last, z + step), (z >= step, z - step)):
@@ -182,43 +181,57 @@
                     send_kv(both(valid, odd), origin, piece, (across(1 << bit), z))
             send_kv(valid, origin, piece, (sibling, z))
 
-    def normed_at(block):
-        begin = pl.multiple_of(lax.rem(block, 2) * rows, rows)
-        return normed_all.at[lax.div(block, 2), pl.ds(begin, rows)]
-
-    def norm_copy(block, way, far=1):
+    chunks = 2 if rows % 32 == 0 else 1
+    chunk_rows = rows // chunks
+
+    def norm_copy(block, way, chunk):
         send_sem = norm_send_up if way > 0 else norm_send_down
+        begin = pl.multiple_of(lax.rem(block, 2) * rows + chunk * chunk_rows, chunk_rows)
+        view = normed_all.at[lax.div(block, 2), pl.ds(begin, chunk_rows)]
+        index = block * chunks + chunk
         return pltpu.make_async_remote_copy(
-            src_ref=normed_at(block),
-            dst_ref=normed_at(block),
-            send_sem=send_sem.at[block if far == 1 else last + far],
-            recv_sem=norm_recv.at[block],
-            device_id=(ctx, z + far * way),
+            src_ref=view,
+            dst_ref=view,
+            send_sem=send_sem.at[index],
+            recv_sem=norm_recv.at[index],
+            device_id=(ctx, z + way),
             device_id_type=MESH,
         )
 
-    def norm_step(step):
-        for valid, block, way, onward in (
+    def norm_blocks(step):
+        return (
             (z >= step, z - step, 1, z < last),
             (z + step <= last, z + step, -1, z > 0),
-        ):
-            copy = norm_copy(block, way)
-            when(valid, copy.wait_recv)
-            when(both(valid, jnp.logical_and(onward, step >= norm_reach)), copy.start)
+        )
+
+    def norm_forward(step):
+        for chunk in range(chunks):
+            for valid, block, way, onward in norm_blocks(step):
+                copy = norm_copy(block, way, chunk)
+                when(both(valid, onward), copy.wait_recv)
+                when(both(valid, onward), copy.start)
+
+    def norm_take(step):
+        for chunk in range(chunks):
+            for valid, block, way, onward in norm_blocks(step):
+                here = jnp.logical_and(valid, jnp.logical_not(onward))
+                when(here, norm_copy(block, way, chunk).wait_recv)
 
     own_block(0)
     loads[1].wait()
     loads[2].wait()
     query_f32 = query_ref[...].astype(jnp.float32)
-    normed_at(z)[...] = (
+    own_row = pl.multiple_of(lax.rem(z, 2) * rows, rows)
+    normed_all[lax.div(z, 2), pl.ds(own_row, rows)] = (
         query_f32
         * lax.rsqrt(jnp.mean(query_f32 * query_f32, axis=-1, keepdims=True) + epsilon)
         * gain_ref[...].reshape(1, -1).astype(jnp.float32)
     ).astype(jnp.bfloat16)
 
-    for far in range(1, norm_reach + 1):
-        when(z + far <= last, norm_copy(z, 1, far).start)
-        when(z >= far, norm_copy(z, -1, far).start)
+    def send_norm():
+        for chunk in range(chunks):
+            when(z < last, norm_copy(z, 1, chunk).start)
+            when(z > 0, norm_copy(z, -1, chunk).start)
 
     def half_base(owner, upper):
         return jnp.where(upper, 2 * ctx_count - 1 - owner, owner) * half_len
@@ -263,9 +276,13 @@
             if 0 <= stage - level < head_devices:
                 for relative in distances[level]:
                     relay(stage - level, relative)
+            if stage == last + level == last + 1:
+                norm_forward(1)
         if stage == 0:
             tables()
-    norm_step(1)
+        if stage == min(kv_reach, last):
+            send_norm()
+    norm_take(1)
     for load in loads[3:]:
         load.wait()
 
@@ -304,9 +321,6 @@
         for piece in range(head_devices):
             wait_kv(True, other_core(across(relative)), piece)
 
-    if last > 1:
-        norm_step(2)
-
     def pair_body(step, carry):
         pair = pair_at(step)
         offset = pair * pair_rows
@@ -335,6 +349,11 @@
             if upper:
                 parts.append(score(rows_of(0)))
                 peak = jnp.maximum(peak, jnp.max(parts[1], axis=-1, keepdims=True))
+
+            @pl.when(jnp.logical_and(step == 0, last > 1))
+            def _():
+                norm_forward(2)
+
             total, weighted = 0.0, 0.0
             for half, part in zip((int(upper), 0), parts):
                 weights = jnp.exp2((part - peak) * factor)
@@ -357,11 +376,10 @@
 
         @pl.when(step < last_pair)
         def _():
-            norm_step(2 * step + 3)
-
-            @pl.when(2 * step + 4 <= last)
-            def _():
-                norm_step(2 * step + 4)
+            norm_take(2 * step + 2)
+            for further in (2 * step + 3, 2 * step + 4):
+                norm_forward(further)
+            norm_take(2 * step + 3)
 
             project(pair_at(step + 1))
 
@@ -371,12 +389,10 @@
 
     for condition, copy in sent:
         when(condition, copy.wait_send)
-    for far in range(1, norm_reach + 1):
-        when(z + far <= last, norm_copy(z, 1, far).wait_send)
-        when(z >= far, norm_copy(z, -1, far).wait_send)
-    for step in range(norm_reach, last):
-        when(both(z >= step, z < last), norm_copy(z - step, 1).wait_send)
-        when(both(z + step <= last, z > 0), norm_copy(z + step, -1).wait_send)
+    for step in range(last):
+        for chunk in range(chunks):
+            when(both(z >= step, z < last), norm_copy(z - step, 1, chunk).wait_send)
+            when(both(z + step <= last, z > 0), norm_copy(z + step, -1, chunk).wait_send)
 
 
 def per_device(query_latent, norm_gain, kv_latent, q_up, absorb_key, absorb_value, block_owner):
@@ -413,9 +429,9 @@
             pltpu.VMEM((2 * head_count * rows, kv_width), bf16),
             pltpu.SemaphoreType.DMA((piece_count,)),
             pltpu.SemaphoreType.DMA((slots,)),
-            pltpu.SemaphoreType.DMA((head_devices,)),
-            pltpu.SemaphoreType.DMA((head_devices + 2,)),
-            pltpu.SemaphoreType.DMA((head_devices + 2,)),
+            pltpu.SemaphoreType.DMA((2 * head_devices,)),
+            pltpu.SemaphoreType.DMA((2 * head_devices,)),
+            pltpu.SemaphoreType.DMA((2 * head_devices,)),
             pltpu.SemaphoreType.DMA((6,)),
         ],
         compiler_params=pltpu.CompilerParams(

time: 40.5 us -> 40.5 us (level)
  no operation moved by 1% of the time
where the time goes in v7:
time: 40.5 us; the launch traced here: 40.3 us
  Pallas kernels  38.6 us (95%)
  local copies, waits for them, and re-layouts  1.67 us (4%)
    pallas_call x1, Pallas kernels, per_device(): pl.pallas_call(functools.partial(kernel, ctx_count, head_devices), out_sh...  38.6 us
    unnamed x1, local copies, waits for them, and re-layouts  1.67 us

profile of v7, /device:TPU:0, one launch (start us, length us, event | category | flops | bytes accessed | tf_op | source)
XLA Modules:
  0.0 40.3 jit_solution(12935136853118001049)
XLA Ops:
  0.0 38.6 %shard_map.73 = bf16[2,128,512]{2,1,0:T(8,128)(2,1)} custom-call(s32[8]{0:T(128)} %owner_ref.1, bf16[64,1536]{1,0:T(8,128)(2,1)} %query_hbm.1, bf16[1536]{0:T(1024)(128)(2,1)} %gain_hbm.1, bf16[64,576]{1,0:T(8,128)(2,1)} %kv_hbm.1, bf16[1536,768]{1,0:T(8,128)(2,1)} %q_up_hbm.1, bf16[4,128,512]{2,1,0:T(8,128)(2,1)} %absorb_key_hbm.1, ...), custom_call_target="tpu_custom_call" | custom-call | tf_op jit(solution)/shard_map/pallas_call | solution.py:412
  38.6 1.7 %copy.9 = bf16[256,512]{1,0:T(8,128)(2,1)} copy(bf16[256,512]{1,0:T(8,128)(2,1)} %bitcast.1) | data formatting | bytes 524288

commit v8 on v7

--- a/solution.py
+++ b/solution.py
@@ -204,8 +204,8 @@
             (z + step <= last, z + step, -1, z > 0),
         )
 
-    def norm_forward(step):
-        for chunk in range(chunks):
+    def norm_forward(step, some=range(chunks)):
+        for chunk in some:
             for valid, block, way, onward in norm_blocks(step):
                 copy = norm_copy(block, way, chunk)
                 when(both(valid, onward), copy.wait_recv)
@@ -228,10 +228,12 @@
         * gain_ref[...].reshape(1, -1).astype(jnp.float32)
     ).astype(jnp.bfloat16)
 
-    def send_norm():
-        for chunk in range(chunks):
+    def send_norm(some):
+        for chunk in some:
             when(z < last, norm_copy(z, 1, chunk).start)
             when(z > 0, norm_copy(z, -1, chunk).start)
+
+    send_norm(range(1))
 
     def half_base(owner, upper):
         return jnp.where(upper, 2 * ctx_count - 1 - owner, owner) * half_len
@@ -272,16 +274,18 @@
     for stage in range(head_devices + bits):
         if 0 < stage < head_devices:
             own_block(stage)
+        if stage == min(kv_reach, last):
+            send_norm(range(1, chunks))
         for level in range(1, bits + 1):
             if 0 <= stage - level < head_devices:
                 for relative in distances[level]:
                     relay(stage - level, relative)
             if stage == last + level == last + 1:
-                norm_forward(1)
+                norm_forward(1, range(1, chunks))
         if stage == 0:
             tables()
-        if stage == min(kv_reach, last):
-            send_norm()
+        if stage == last:
+            norm_forward(1, range(1))
     norm_take(1)
     for load in loads[3:]:
         load.wait()
@@ -321,6 +325,9 @@
         for piece in range(head_devices):
             wait_kv(True, other_core(across(relative)), piece)
 
+    if last > 1:
+        norm_forward(2, range(1))
+
     def pair_body(step, carry):
         pair = pair_at(step)
         offset = pair * pair_rows
@@ -352,7 +359,7 @@
 
             @pl.when(jnp.logical_and(step == 0, last > 1))
             def _():
-                norm_forward(2)
+                norm_forward(2, range(1, chunks))
 
             total, weighted = 0.0, 0.0
             for half, part in zip((int(upper), 0), parts):

time: 40.5 us -> 38.2 us (0.943)
  Pallas kernels: 38.6 us -> 36.4 us
    pallas_call x1, Pallas kernels: 38.6 us -> 36.4 us  [per_device(): pl.pallas_call(functools.partial(kernel, ctx_count, head_devices), out_sh...]
where the time goes in v8:
time: 38.2 us; the launch traced here: 38.1 us
  Pallas kernels  36.4 us (95%)
  local copies, waits for them, and re-layouts  1.67 us (4%)
    pallas_call x1, Pallas kernels, per_device(): pl.pallas_call(functools.partial(kernel, ctx_count, head_devices), out_sh...  36.4 us
    unnamed x1, local copies, waits for them, and re-layouts  1.67 us

profile of v8, /device:TPU:0, one launch (start us, length us, event | category | flops | bytes accessed | tf_op | source)
XLA Modules:
  0.0 38.1 jit_solution(10827222021359365533)
XLA Ops:
  0.0 36.4 %shard_map.73 = bf16[2,128,512]{2,1,0:T(8,128)(2,1)} custom-call(s32[8]{0:T(128)} %owner_ref.1, bf16[64,1536]{1,0:T(8,128)(2,1)} %query_hbm.1, bf16[1536]{0:T(1024)(128)(2,1)} %gain_hbm.1, bf16[64,576]{1,0:T(8,128)(2,1)} %kv_hbm.1, bf16[1536,768]{1,0:T(8,128)(2,1)} %q_up_hbm.1, bf16[4,128,512]{2,1,0:T(8,128)(2,1)} %absorb_key_hbm.1, ...), custom_call_target="tpu_custom_call" | custom-call | tf_op jit(solution)/shard_map/pallas_call | solution.py:419
  36.4 1.7 %copy.9 = bf16[256,512]{1,0:T(8,128)(2,1)} copy(bf16[256,512]{1,0:T(8,128)(2,1)} %bitcast.1) | data formatting | bytes 524288

commit v9 on v8

--- a/solution.py
+++ b/solution.py
@@ -276,6 +276,8 @@
             own_block(stage)
         if stage == min(kv_reach, last):
             send_norm(range(1, chunks))
+        if stage == last:
+            norm_forward(1, range(1))
         for level in range(1, bits + 1):
             if 0 <= stage - level < head_devices:
                 for relative in distances[level]:
@@ -284,8 +286,6 @@
                 norm_forward(1, range(1, chunks))
         if stage == 0:
             tables()
-        if stage == last:
-            norm_forward(1, range(1))
     norm_take(1)
     for load in loads[3:]:
         load.wait()

time: 38.2 us -> 37.6 us (0.984)
  Pallas kernels: 36.4 us -> 35.7 us
    pallas_call x1, Pallas kernels: 36.4 us -> 35.7 us  [per_device(): pl.pallas_call(functools.partial(kernel, ctx_count, head_devices), out_sh...]
where the time goes in v9:
time: 37.6 us; the launch traced here: 37.4 us
  Pallas kernels  35.7 us (95%)
  local copies, waits for them, and re-layouts  1.67 us (4%)
    pallas_call x1, Pallas kernels, per_device(): pl.pallas_call(functools.partial(kernel, ctx_count, head_devices), out_sh...  35.7 us
    unnamed x1, local copies, waits for them, and re-layouts  1.67 us

profile of v9, /device:TPU:0, one launch (start us, length us, event | category | flops | bytes accessed | tf_op | source)
XLA Modules:
  0.0 37.4 jit_solution(6372889394176641698)
XLA Ops:
  0.0 35.7 %shard_map.73 = bf16[2,128,512]{2,1,0:T(8,128)(2,1)} custom-call(s32[8]{0:T(128)} %owner_ref.1, bf16[64,1536]{1,0:T(8,128)(2,1)} %query_hbm.1, bf16[1536]{0:T(1024)(128)(2,1)} %gain_hbm.1, bf16[64,576]{1,0:T(8,128)(2,1)} %kv_hbm.1, bf16[1536,768]{1,0:T(8,128)(2,1)} %q_up_hbm.1, bf16[4,128,512]{2,1,0:T(8,128)(2,1)} %absorb_key_hbm.1, ...), custom_call_target="tpu_custom_call" | custom-call | tf_op jit(solution)/shard_map/pallas_call | solution.py:419
  35.7 1.7 %copy.9 = bf16[256,512]{1,0:T(8,128)(2,1)} copy(bf16[256,512]{1,0:T(8,128)(2,1)} %bitcast.1) | data formatting | bytes 524288
